TPU v7x, 512 devices: a whole 4x8x8 slice. The times are simulated.
512 devices in a mesh: ax: 32 (over y_lo, z), sec: 16 (over x, y_hi, core).
Axes of the slice: x: 4, y: 8 (y_hi: 2, y_lo: 4; y = y_hi * 4 + y_lo), z: 8, core: 2. Of those that a mesh axis runs over, the one named last changes fastest.
Arguments:
- balance_quantities: float32 [5, 128, 512, 128], P(None, 'ax', 'sec'), may hold values from -0.75 to 3.5, as said below
- register: float32 [5, 128, 512, 128], P(None, 'ax', 'sec'), may hold values from -6 to 6
Outputs:
- conserved_new: float32 [5, 128, 512, 128], P(None, 'ax', 'sec')
- register_new: float32 [5, 128, 512, 128], P(None, 'ax', 'sec')
Inputs may be any that keep to these rules, and one draw needn't show every extreme that they name: `balance_quantities`: component 0 lies in 0.5 to 1.5 and component 4 in 1.5 to 3.5; components 1 to 3 vanish at the first and last radial nodes.
All inputs are finite; a program needn't handle non-finite values.
Results may differ from a plain program's by a relative error of at most 0.0004.
Values sent between devices are 32-bit elements; how exact they have to be, the bound alone decides.
A program may use at most 64 MiB of HBM per device.

v0:
```python
import jax
import jax.numpy as jnp
from jax import lax
from jax.sharding import PartitionSpec as P

HEAT_RATIO = 1.4
AXIAL_STEP = 0.003
INNER_RADIUS = 0.25
TIME_STEP = 0.001
SECTION_DECAY = -5.0 / 9.0
SEGMENT_WEIGHT = 15.0 / 16.0
VISCOSITY = 2.5e-05
CONDUCTION = VISCOSITY / ((HEAT_RATIO - 1.0) * 0.7)
TARGET_BULK = 0.4
FORCE_RATE = 8000.0
FIRST_COEFFS = (4.0 / 5.0, -1.0 / 5.0, 4.0 / 105.0, -1.0 / 280.0)
SECOND_CENTER = -205.0 / 72.0
SECOND_COEFFS = (8.0 / 5.0, -1.0 / 5.0, 8.0 / 315.0, -1.0 / 560.0)
HIGHEST = lax.Precision.HIGHEST


def with_halo(cells, sides, width):
    for axis, dim in sides:
        count = lax.axis_size(axis)
        head = lax.slice_in_dim(cells, 0, width, axis=dim)
        tail = lax.slice_in_dim(cells, cells.shape[dim] - width, cells.shape[dim], axis=dim)
        cells = jnp.concatenate(
            [
                lax.ppermute(tail, axis, [(i, (i + 1) % count) for i in range(count)]),
                cells,
                lax.ppermute(head, axis, [((i + 1) % count, i) for i in range(count)]),
            ],
            axis=dim,
        )
    return cells


def radial_matrix(number_of_shells):
    positions = jnp.arange(number_of_shells)
    nodes = jnp.cos(jnp.pi * positions.astype(jnp.float32) / (number_of_shells - 1))
    radius = 0.5 * (1.0 + INNER_RADIUS) + 0.5 * (1.0 - INNER_RADIUS) * nodes
    row_index = positions[:, None]
    col_index = positions[None, :]
    endpoint = jnp.where((positions == 0) | (positions == number_of_shells - 1), 2.0, 1.0).astype(
        jnp.float32
    )
    parity = jnp.where((row_index + col_index) % 2 == 0, 1.0, -1.0).astype(jnp.float32)
    diagonal = row_index == col_index
    spread = jnp.where(diagonal, 1.0, nodes[:, None] - nodes[None, :])
    offdiag = jnp.where(diagonal, 0.0, endpoint[:, None] / endpoint[None, :] * parity / spread)
    radial_first = (offdiag - jnp.diag(jnp.sum(offdiag, axis=1))) * (2.0 / (1.0 - INNER_RADIUS))
    radial_second = jnp.dot(radial_first, radial_first, precision=HIGHEST)
    return (radius, radial_first, radial_second)


def azimuth_matrices(azim_count):
    positions = jnp.arange(azim_count)
    offset = (positions[:, None] - positions[None, :]) % azim_count
    angle_step = 2.0 * jnp.pi / azim_count
    half_angle = offset.astype(jnp.float32) * angle_step * 0.5
    parity = jnp.where(offset % 2 == 0, 1.0, -1.0).astype(jnp.float32)
    at_zero = offset == 0
    tangent = jnp.tan(jnp.where(at_zero, 1.0, half_angle))
    azim_first = jnp.where(at_zero, 0.0, 0.5 * parity / tangent)
    sine_value = jnp.sin(jnp.where(at_zero, 1.0, half_angle))
    azim_second = jnp.where(
        at_zero,
        -jnp.pi * jnp.pi / (3.0 * angle_step * angle_step) - 1.0 / 6.0,
        -0.5 * parity / (sine_value * sine_value),
    )
    return (azim_first, azim_second)


def physical_variables(balance_quantities):
    specific_volume_inverse = balance_quantities[0]
    motion_vector = balance_quantities[1:4] / specific_volume_inverse
    thermodynamic_stress = (HEAT_RATIO - 1.0) * (
        balance_quantities[4] - 0.5 * jnp.sum(balance_quantities[1:4] * motion_vector, axis=0)
    )
    thermal_state_value = thermodynamic_stress / specific_volume_inverse
    return (specific_volume_inverse, motion_vector, thermodynamic_stress, thermal_state_value)


def transport_rates(balance_quantities, direction):
    specific_volume_inverse, motion_vector, thermodynamic_stress, thermal_state_value = (
        physical_variables(balance_quantities)
    )
    along_speed = motion_vector[direction]
    pieces = [balance_quantities[component] * along_speed for component in range(5)]
    pieces[1 + direction] = pieces[1 + direction] + thermodynamic_stress
    pieces[4] = pieces[4] + thermodynamic_stress * along_speed
    return jnp.stack(pieces)


def transported(balance_quantities):
    specific_volume_inverse, motion_vector, thermodynamic_stress, thermal_state_value = (
        physical_variables(balance_quantities)
    )
    return jnp.concatenate([motion_vector, thermal_state_value[None]], axis=0)


def axial_parts(balance_quantities):
    return jnp.concatenate(
        [transport_rates(balance_quantities, 0), transported(balance_quantities)], axis=0
    )


def azim_parts(balance_quantities):
    return jnp.concatenate(
        [transport_rates(balance_quantities, 1), transported(balance_quantities)], axis=0
    )


def assemble(
    balance_quantities, motion_vector, thermodynamic_stress, convect, lap, forcing, radius
):
    terms = [
        -convect[0],
        -convect[1] + VISCOSITY * lap[0] + forcing,
        -convect[2] - balance_quantities[2] * motion_vector[2] / radius + VISCOSITY * lap[1],
        -convect[3]
        + (balance_quantities[2] * motion_vector[1] + thermodynamic_stress) / radius
        + VISCOSITY * lap[2],
        -convect[4] + CONDUCTION * lap[3] + forcing * motion_vector[0],
    ]
    return jnp.stack(terms)


def first_difference(padded, planes):
    summed = jnp.zeros_like(padded[:, 4 : 4 + planes])
    for offset, weight in enumerate(FIRST_COEFFS, 1):
        summed = summed + weight * (
            padded[:, 4 + offset : 4 + offset + planes]
            - padded[:, 4 - offset : 4 - offset + planes]
        )
    return summed / AXIAL_STEP


def second_difference(padded, planes):
    summed = SECOND_CENTER * padded[:, 4 : 4 + planes]
    for offset, weight in enumerate(SECOND_COEFFS, 1):
        summed = summed + weight * (
            padded[:, 4 + offset : 4 + offset + planes]
            + padded[:, 4 - offset : 4 - offset + planes]
        )
    return summed / (AXIAL_STEP * AXIAL_STEP)


def shards(balance_quantities, register):
    planes = balance_quantities.shape[1]
    sector = balance_quantities.shape[2]
    number_of_shells = balance_quantities.shape[3]
    full_azim = sector * lax.axis_size("sec")
    radius, radial_first, radial_second = radial_matrix(number_of_shells)
    azim_first, azim_second = azimuth_matrices(full_azim)
    padded = with_halo(axial_parts(balance_quantities), (("ax", 1),), 4)
    axial_one = first_difference(padded[:5], planes)
    axial_two = second_difference(padded[5:], planes)
    pieces = lax.all_to_all(
        azim_parts(balance_quantities), "sec", split_axis=3, concat_axis=2, tiled=True
    )
    flux_part = jnp.einsum("ab,cnbi->cnai", azim_first, pieces[:5], precision=HIGHEST)
    diff_part = jnp.einsum("ab,cnbi->cnai", azim_second, pieces[5:], precision=HIGHEST)
    derived = jnp.concatenate([flux_part, diff_part], axis=0)
    turned = lax.all_to_all(derived, "sec", split_axis=2, concat_axis=3, tiled=True)
    stacked = jnp.concatenate(
        [transport_rates(balance_quantities, 2) * radius, transported(balance_quantities)], axis=0
    )
    radial_one = jnp.dot(stacked, radial_first.T, precision=HIGHEST)
    radial_two = jnp.dot(stacked[5:], radial_second.T, precision=HIGHEST)
    local_flow = jnp.sum(balance_quantities[1] * radius)
    bulk_mean = lax.psum(local_flow, ("ax", "sec")) / (
        planes * lax.axis_size("ax") * full_azim * jnp.sum(radius)
    )
    forcing = FORCE_RATE * (TARGET_BULK - bulk_mean)
    specific_volume_inverse, motion_vector, thermodynamic_stress, thermal_state_value = (
        physical_variables(balance_quantities)
    )
    convect = axial_one + (radial_one[:5] / radius + turned[:5] / radius)
    lap = radial_two + radial_one[5:] / radius + turned[5:] / (radius * radius) + axial_two
    tendency = assemble(
        balance_quantities, motion_vector, thermodynamic_stress, convect, lap, forcing, radius
    )
    register_new = SECTION_DECAY * register + TIME_STEP * tendency
    conserved_new = balance_quantities + SEGMENT_WEIGHT * register_new
    return (conserved_new, register_new)


def solution(mesh):
    return jax.shard_map(
        shards,
        mesh=mesh,
        in_specs=(P(None, "ax", "sec", None), P(None, "ax", "sec", None)),
        out_specs=(P(None, "ax", "sec", None), P(None, "ax", "sec", None)),
        check_vma=False,
    )
```

profile of v0, /device:TPU:1, one launch (start us, length us, event | category | flops | bytes accessed | tf_op | source)
XLA Modules:
  0.0 226.0 jit_solution(12441126489581138537)
XLA Ops:
  0.6 0.9 slice_bitcast_fusion.2
  1.6 1.0 multiply_reduce_fusion
  2.5 0.9 multiply_dynamic-update-slice_fusion.7
  3.4 0.9 multiply_dynamic-update-slice_fusion.6
  4.3 0.6 add_dynamic-update-slice_fusion
  5.0 0.7 multiply_dynamic-update-slice_fusion.1
  5.6 0.7 multiply_dynamic-update-slice_fusion.9
  6.3 0.6 multiply_dynamic-update-slice_fusion.8
  7.0 0.7 constant_dynamic-update-slice_fusion.3
  7.6 1.4 copy.21
  9.1 2.3 %reshape.76 = f32[16,1,9216]{2,1,0:T(1,128)} reshape(f32[128,9,4,32]{3,2,1,0:T(4,128)S(1)} %bitcast.64) | data formatting | bytes 1179648
  11.4 11.2 %all-to-all-start = ((f32[16,1,9216]{2,1,0:T(1,128)}), f32[16,1,9216]{2,1,0:T(1,128)S(1)}, u32[]{:S(2)}, u32[]{:S(2)}) async-start(f32[16,1,9216]{2,1,0:T(1,128)} %reshape.76), calls=%async_computation | async-start | bytes 1179648 | tf_op jit(solution)/shard_map/all_to_all | solution.py:159
  22.6 0.7 constant_dynamic-update-slice_fusion.1
  23.3 0.6 constant_dynamic-update-slice_fusion
  24.0 11.0 %collective-permute-start = (f32[9,4,32,128]{3,2,1,0:T(8,128)}, f32[9,4,32,128]{3,2,1,0:T(8,128)}, u32[]{:S(2)}, u32[]{:S(2)}) collective-permute-start(f32[9,4,32,128]{3,2,1,0:T(8,128)} %constant_dynamic-update-slice_fusion), channel_id=1, source_target_pairs={{16,0},{32,16},{48,32},{64,48},{80,64},{96,80},{112,96},{128,112},... | collective-permute-start | bytes 1769480 | tf_op jit(solution)/shard_map/ppermute | solution.py:31
  35.0 2.1 collective-permute-start.1
  37.1 2.2 all-to-all-done
  39.3 0.5 broadcast.198
  39.8 2.0 reduce
  41.8 1.2 reshape.77
  43.1 0.3 copy.34
  43.4 0.1 slice.275
  43.6 0.2 copy.23
  43.8 1.2 slice.232
  45.1 6.6 %convolution_bitcast_fusion = f32[5,4,512,8]{2,3,1,0:T(8,128)S(1)} fusion(f32[5,4,512,8]{2,3,1,0:T(8,128)} %slice.232), kind=kOutput, calls=%fused_computation.30 | convolution fusion | flops 511705088 | bytes 655360 | tf_op jit(solution)/shard_map/ab,cnbi->cnai/dot_general | solution.py:162
  51.6 0.2 copy.24
  51.8 0.4 slice.234
  52.3 6.2 %convolution_bitcast_fusion.1 = f32[4,4,512,8]{2,3,1,0:T(8,128)S(1)} fusion(f32[4,4,512,8]{2,3,1,0:T(8,128)S(1)} %slice.234), kind=kOutput, calls=%fused_computation.33 | convolution fusion | flops 411303936 | bytes 524288 | tf_op jit(solution)/shard_map/ab,cnbi->cnai/dot_general | solution.py:163
  58.5 7.6 %copy.25 = f32[9,4,512,8]{0,3,1,2:T(8,128)} copy(f32[9,4,512,8]{2,3,1,0:T(8,128)S(1)} %pad_maximum_fusion) | data formatting | bytes 1179648 | tf_op jit(solution)/shard_map/concatenate | solution.py:164
  66.1 8.6 %reshape.78 = f32[16,1,9216]{2,1,0:T(1,128)} reshape(f32[512,4,8,9]{3,2,1,0:T(8,128)} %bitcast.60) | data formatting | bytes 1179648
  74.7 7.9 %all-to-all-start.1 = ((f32[16,1,9216]{2,1,0:T(1,128)}), f32[16,1,9216]{2,1,0:T(1,128)S(1)}, u32[]{:S(2)}, u32[]{:S(2)}) async-start(f32[16,1,9216]{2,1,0:T(1,128)} %reshape.78), calls=%async_computation.1 | async-start | bytes 1179648 | tf_op jit(solution)/shard_map/all_to_all | solution.py:165
  82.7 0.6 fusion.97
  83.4 0.2 fusion.109
  83.5 1.0 convolution_bitcast_fusion.2
  84.6 1.5 fusion.20
  86.2 106.9 %psum.7 = f32[]{:T(128)} all-reduce(f32[]{:T(128)} %fusion.97), channel_id=1, replica_groups=mesh['ax'=32,'sec'=16] {'ax','sec'}, use_global_device_ids=true, to_apply=%region_3.4 | all-reduce | flops 1 | bytes 8 | tf_op jit(solution)/shard_map/psum | solution.py:172
  193.1 0.7 fusion.110
  195.0 2.0 reduce.1
  197.1 10.8 %reshape.79 = f32[512,4,8,9]{3,2,1,0:T(8,128)} reshape(f32[16,9216]{1,0:T(8,128)S(1)} %reduce.1) | data formatting | bytes 1179648
  207.9 6.1 %copy.26 = f32[9,4,16,32,8]{3,4,2,1,0:T(8,128)S(1)} copy(f32[9,4,16,32,8]{0,4,1,3,2:T(8,128)} %bitcast.61) | data formatting | bytes 1179648 | tf_op jit(solution)/shard_map/all_to_all | solution.py:165
  214.0 1.0 slice_bitcast_fusion.1
  215.0 1.5 copy.28
  216.6 1.2 slice_bitcast_fusion
  217.7 1.7 copy.27
  219.5 2.3 %fusion.45 = f32[5,4,32,128]{3,2,1,0:T(8,128)S(1)} fusion(f32[9,4,32,128]{3,2,1,0:T(8,128)} %collective-permute-done.1, f32[9,4,32,128]{3,2,1,0:T(8,128)} %constant_dynamic-update-slice_fusion, f32[9,4,32,128]{3,2,1,0:T(8,128)} %collective-permute-done, f32[9,4,32,128]{3,2,1,0:T(8,128)S(1)} %copy-done.6, f32[5,4,32,128]{3,2,1,0:T(8,128)S(1)} %copy.27, ...), kind=kLoop, calls=%fused_computation.79 | loop fusion | flops 1802240 | bytes 3408384 | tf_op jit(solution)/shard_map/add | solution.py:179
  221.9 2.2 fusion.64
  224.2 0.8 copy-done.3
  225.1 0.9 multiply_add_fusion
  (32 shorter events, 0.5 us)
Async XLA Ops:
  0.6 3.6 %copy-start = (f32[5,4,32,128]{3,2,1,0:T(8,128)S(1)}, f32[5,4,32,128]{3,2,1,0:T(8,128)}, u32[]{:S(2)}) copy-start(f32[5,4,32,128]{3,2,1,0:T(8,128)} %param.2) | copy-start | bytes 983044
  5.6 2.0 copy-start.1
  11.4 11.9 %copy-start.4 = (f32[1,4,32,128]{3,2,1,0:T(8,128)S(1)}, f32[1,4,32,128]{3,2,1,0:T(8,128)}, u32[]{:S(2)}) copy-start(f32[1,4,32,128]{3,2,1,0:T(8,128)} %get-tuple-element.5) | copy-start | bytes 196612
  11.4 27.8 %all-to-all-start = ((f32[16,1,9216]{2,1,0:T(1,128)}), f32[16,1,9216]{2,1,0:T(1,128)S(1)}, u32[]{:S(2)}, u32[]{:S(2)}) async-start(f32[16,1,9216]{2,1,0:T(1,128)} %reshape.76), calls=%async_computation | async-start | bytes 1179648 | tf_op jit(solution)/shard_map/all_to_all | solution.py:159
  24.0 195.5 %collective-permute-start = (f32[9,4,32,128]{3,2,1,0:T(8,128)}, f32[9,4,32,128]{3,2,1,0:T(8,128)}, u32[]{:S(2)}, u32[]{:S(2)}) collective-permute-start(f32[9,4,32,128]{3,2,1,0:T(8,128)} %constant_dynamic-update-slice_fusion), channel_id=1, source_target_pairs={{16,0},{32,16},{48,32},{64,48},{80,64},{96,80},{112,96},{128,112},... | collective-permute-start | bytes 1769480 | tf_op jit(solution)/shard_map/ppermute | solution.py:31
  35.0 184.5 %collective-permute-start.1 = (f32[9,4,32,128]{3,2,1,0:T(8,128)}, f32[9,4,32,128]{3,2,1,0:T(8,128)}, u32[]{:S(2)}, u32[]{:S(2)}) collective-permute-start(f32[9,4,32,128]{3,2,1,0:T(8,128)} %constant_dynamic-update-slice_fusion), channel_id=1, source_target_pairs={{0,16},{16,32},{32,48},{48,64},{64,80},{80,96},{96,112},{112,128},... | collective-permute-start | bytes 1769480 | tf_op jit(solution)/shard_map/ppermute | solution.py:29
  74.7 9.8 %copy-start.2 = (f32[5,4,32,128]{3,2,1,0:T(8,128)S(1)}, f32[5,4,32,128]{3,2,1,0:T(8,128)}, u32[]{:S(2)}) copy-start(f32[5,4,32,128]{3,2,1,0:T(8,128)} %copy-done.1) | copy-start | bytes 983044
  74.7 9.8 %copy-start.5 = (f32[1,4,32,128]{3,2,1,0:T(8,128)S(1)}, f32[1,4,32,128]{3,2,1,0:T(8,128)}, u32[]{:S(2)}) copy-start(f32[1,4,32,128]{3,2,1,0:T(8,128)} %get-tuple-element.5) | copy-start | bytes 196612
  74.7 120.3 %all-to-all-start.1 = ((f32[16,1,9216]{2,1,0:T(1,128)}), f32[16,1,9216]{2,1,0:T(1,128)S(1)}, u32[]{:S(2)}, u32[]{:S(2)}) async-start(f32[16,1,9216]{2,1,0:T(1,128)} %reshape.78), calls=%async_computation.1 | async-start | bytes 1179648 | tf_op jit(solution)/shard_map/all_to_all | solution.py:165
  217.7 1.8 copy-start.6
  219.5 2.4 %copy-start.7 = (f32[128,128,1,1]{1,0,3,2:T(8,128)S(1)}, f32[128,128,1,1]{1,0,3,2:T(8,128)}, u32[]{:S(2)}) copy-start(f32[128,128,1,1]{1,0,3,2:T(8,128)} %convolution_bitcast_fusion.2) | copy-start | bytes 196612
  224.1 1.0 copy-start.3
where the time goes:
time: 227 us; the launch traced here: 226 us
  blocking collectives  107 us (47%)
  local copies, waits for them, and re-layouts  49.9 us (22%)
  starting transfers between devices  32.2 us (14%)
  matrix products  17.5 us (8%)
  other arithmetic  15.1 us (7%)
    psum x1, blocking collectives, shards(): lax.psum(local_flow, ('ax', 'sec'))  107 us
    unnamed x22, local copies, waits for them, and re-layouts  24.6 us
    all_to_all x1, starting transfers between devices, shards(): lax.all_to_all(azim_parts(balance_quantities), 'sec', split_axis=3, conca...  11.2 us
    ppermute x1, starting transfers between devices, with_halo(): lax.ppermute(head, axis, [((i + 1) % count, i) for i in range(count)])  11 us
    all_to_all x1, starting transfers between devices, shards(): lax.all_to_all(derived, 'sec', split_axis=2, concat_axis=3, tiled=True)  7.88 us
    concatenate x1, local copies, waits for them, and re-layouts, shards(): derived = jnp.concatenate([flux_part, diff_part], axis=0)  7.62 us
    dot_general x1, matrix products, shards(): jnp.einsum('ab,cnbi->cnai', azim_first, pieces[:5], precision=HIGHEST)  6.58 us
    dot_general x1, matrix products, shards(): jnp.einsum('ab,cnbi->cnai', azim_second, pieces[5:], precision=HIGHEST)  6.18 us
  transfers between devices with their start and end apart: 4, of which 1 were waited for; matrix products, arithmetic and copies ran while one was open for 29% of the time, Pallas kernels for 0%

commit v1 on v0

v1 whole, which is shorter than its diff:
```python
import functools

import jax
import jax.numpy as jnp
import ml_dtypes
import numpy as np
from jax import lax
from jax.experimental import pallas as pl
from jax.experimental.pallas import tpu as pltpu
from jax.sharding import PartitionSpec as P

AXIAL_STEP = 0.003
TIME_STEP = 0.001
SECTION_DECAY = -5.0 / 9.0
SEGMENT_WEIGHT = 15.0 / 16.0
VISCOSITY = 2.5e-05
CONDUCTION = VISCOSITY / (0.4 * 0.7)
TARGET_BULK = 0.4
FORCE_RATE = 8000.0
FIRST_COEFFS = (4.0 / 5.0, -1.0 / 5.0, 4.0 / 105.0, -1.0 / 280.0)
SECOND_CENTER = -205.0 / 72.0
SECOND_COEFFS = (8.0 / 5.0, -1.0 / 5.0, 8.0 / 315.0, -1.0 / 560.0)
HIGHEST = lax.Precision.HIGHEST
MESH = pl.DeviceIdType.MESH

R = 128
NTH = 512
NZ = 128
NSEC = 16
NAX = 32
F32 = jnp.float32
BF16 = jnp.bfloat16


def constants():
    index = np.arange(R)
    nodes = np.cos(np.pi * index / (R - 1))
    radius = 0.625 + 0.375 * nodes
    ends = np.where((index == 0) | (index == R - 1), 2.0, 1.0)
    spread = nodes[:, None] - nodes[None, :]
    np.fill_diagonal(spread, 1.0)
    parity = np.where((index[:, None] + index[None, :]) % 2 == 0, 1.0, -1.0)
    off = ends[:, None] / ends[None, :] * parity / spread
    np.fill_diagonal(off, 0.0)
    first = (off - np.diag(off.sum(axis=1))) * (2.0 / 0.75)
    second = first @ first

    lag = (np.arange(NTH)[:, None] - np.arange(NTH)[None, :]) % NTH
    step = 2.0 * np.pi / NTH
    sign = np.where(lag % 2 == 0, 1.0, -1.0)
    safe = np.where(lag == 0, 1, lag)
    azim_first = np.where(lag == 0, 0.0, 0.5 * sign / np.tan(safe * step / 2))
    azim_second = np.where(
        lag == 0,
        -np.pi * np.pi / (3.0 * step * step) - 1.0 / 6.0,
        -0.5 * sign / np.sin(safe * step / 2) ** 2,
    )
    order = (
        np.arange(NTH).reshape(NSEC, 4, 8).transpose(1, 0, 2).reshape(NTH)
    )
    both = np.concatenate(
        [azim_first[order][:, order], azim_second[order][:, order]], axis=1
    )
    both = both.astype(np.float32)
    high = both.astype(ml_dtypes.bfloat16)
    low = (both - high.astype(np.float32)).astype(ml_dtypes.bfloat16)

    flux_op = -TIME_STEP * (first * radius[None, :]) / radius[:, None]
    diff_op = TIME_STEP * (second + first / radius[:, None])
    radial = np.stack(
        [flux_op.T, VISCOSITY * diff_op.T, CONDUCTION * diff_op.T]
    ).astype(np.float32)

    rows = np.zeros((8, R), np.float32)
    rows[0] = radius
    rows[1] = 1.0 / radius
    quarter = np.zeros((4, 8, R), np.float32)
    for q in range(4):
        own = np.tile(radius[32 * q : 32 * q + 32], 4)
        quarter[q, 0] = -TIME_STEP / own
        quarter[q, 1] = TIME_STEP * VISCOSITY / own**2
        quarter[q, 2] = TIME_STEP * CONDUCTION / own**2
    scale = 1.0 / (NZ * NTH * radius.sum())
    return high, low, radial, rows, quarter, float(scale)


def block_transpose(v, lane):
    v0, v1, v2, v3 = v
    low = lane < 64
    even = (lane // 32) % 2 == 0

    def swap(a, b, mask, shift):
        return (
            jnp.where(mask, a, pltpu.roll(b, shift, 1)),
            jnp.where(mask, pltpu.roll(a, 128 - shift, 1), b),
        )

    a0, a2 = swap(v0, v2, low, 64)
    a1, a3 = swap(v1, v3, low, 64)
    b0, b1 = swap(a0, a1, even, 32)
    b2, b3 = swap(a2, a3, even, 32)
    return b0, b1, b2, b3


def physical(q):
    inverse = 1.0 / q[0]
    v = [q[1] * inverse, q[2] * inverse, q[3] * inverse]
    pressure = 0.4 * (q[4] - 0.5 * (q[1] * v[0] + q[2] * v[1] + q[3] * v[2]))
    return v, pressure, pressure * inverse


def flux(q, v, pressure, direction):
    w = v[direction]
    out = [q[1 + direction], q[1] * w, q[2] * w, q[3] * w, (q[4] + pressure) * w]
    out[1 + direction] = out[1 + direction] + pressure
    return out


def split(x):
    high = x.astype(BF16)
    return high, (x - high.astype(F32)).astype(BF16)


def body(
    scale,
    q_ref,
    high_hbm,
    low_hbm,
    radial_ref,
    rows_ref,
    quarter_ref,
    out_ref,
    high,
    low,
    pack,
    recv,
    send,
    back,
    halo,
    sums,
    pairs,
    totals,
    load_sem,
    a_send,
    a_recv,
    s_send,
    s_recv,
    p_send,
    p_recv,
    b_send,
    b_recv,
    t_send,
    t_recv,
    h_send,
    h_recv,
):
    ax = lax.axis_index("ax")
    sec = lax.axis_index("sec")
    loads = [
        pltpu.make_async_copy(high_hbm, high, load_sem.at[0]),
        pltpu.make_async_copy(low_hbm, low, load_sem.at[1]),
    ]
    for copy in loads:
        copy.start()

    def remote(src, dst, send_sem, recv_sem, to_ax, to_sec):
        return pltpu.make_async_remote_copy(
            src_ref=src,
            dst_ref=dst,
            send_sem=send_sem,
            recv_sem=recv_sem,
            device_id=(to_ax, to_sec),
            device_id_type=MESH,
        )

    right = lax.rem(ax + 1, NAX)
    left = lax.rem(ax + NAX - 1, NAX)
    near, far = 2 * sec + 1, 2 * sec + 2
    last = sec == NSEC - 1

    barrier = pltpu.get_barrier_semaphore()

    def greet(to_ax, to_sec):
        pl.semaphore_signal(
            barrier, inc=1, device_id=(to_ax, to_sec), device_id_type=MESH
        )

    peers = [lax.rem(sec + d, NSEC) for d in range(1, NSEC)]
    for peer in peers:
        greet(ax, peer)
    greet(left, sec)
    greet(right, sec)
    greet(lax.rem(ax + near, NAX), sec)

    @pl.when(jnp.logical_not(last))
    def _():
        greet(lax.rem(ax + far, NAX), sec)

    lane = lax.broadcasted_iota(jnp.int32, (1, 128), 1)
    groups = [
        q_ref[:, :, 8 * g : 8 * g + 8, :].reshape(160, 128) for g in range(4)
    ]
    for quarter, packed in enumerate(block_transpose(groups, lane)):
        packed = packed.reshape(5, 4, 8, 128)
        for plane in range(4):
            pack[4 * plane + quarter] = packed[:, plane]

    radius = rows_ref[0:1, :]
    flow = jnp.sum(q_ref[1].reshape(128, 128) * radius, axis=0, keepdims=True)
    sums[sec] = flow

    pl.semaphore_wait(barrier, jnp.where(last, 18, 19))

    first = []
    for d, peer in enumerate(peers):
        first.append(
            remote(sums.at[sec], sums.at[sec], s_send.at[d], s_recv.at[d], ax, peer)
        )
        first.append(
            remote(pack.at[peer], recv.at[sec], a_send.at[d], a_recv.at[d], ax, peer)
        )
    for copy in first:
        copy.start()
    recv[sec] = pack[sec]
    halos = [
        remote(q_ref, halo.at[0], h_send.at[0], h_recv.at[0], right, sec),
        remote(q_ref, halo.at[1], h_send.at[1], h_recv.at[1], left, sec),
    ]
    for copy in halos:
        copy.start()

    whole = [q_ref[c].reshape(128, 128) for c in range(5)]
    v, pressure, heat = physical(whole)
    inverse_radius = rows_ref[1:2, :]
    diffused = v + [heat]
    tend = []
    for c, field in enumerate(flux(whole, v, pressure, 2)):
        value = jnp.dot(
            field, radial_ref[0], precision=HIGHEST, preferred_element_type=F32
        )
        if c:
            value = value + jnp.dot(
                diffused[c - 1],
                radial_ref[2 if c == 4 else 1],
                precision=HIGHEST,
                preferred_element_type=F32,
            )
        tend.append(value)
    turn = TIME_STEP * inverse_radius
    tend[2] = tend[2] - whole[2] * v[2] * turn
    tend[3] = tend[3] + (whole[2] * v[1] + pressure) * turn
    for c in range(5):
        out_ref[c] = tend[c].reshape(4, 32, 128)

    for copy in first[0::2]:
        copy.wait_recv()
    slab = sums[0]
    for s in range(1, NSEC):
        slab = slab + sums[s]
    pairs[0] = slab
    ring_near = remote(
        pairs.at[0],
        pairs.at[1],
        p_send.at[0],
        p_recv.at[0],
        lax.rem(ax + NAX - near, NAX),
        sec,
    )
    ring_far = remote(
        pairs.at[0],
        pairs.at[2],
        p_send.at[1],
        p_recv.at[1],
        lax.rem(ax + 2 * NAX - far, NAX),
        sec,
    )
    ring_near.start()

    @pl.when(jnp.logical_not(last))
    def _():
        ring_far.start()

    for copy in loads:
        copy.wait()
    for copy in first[1::2]:
        copy.wait_recv()
    lines = [recv[:, c].reshape(128, 128) for c in range(5)]
    v, pressure, heat = physical(lines)
    mine = quarter_ref[lax.rem(sec, 4)]
    fields = [f * mine[0:1] for f in flux(lines, v, pressure, 1)]
    viscous = [u * mine[1:2] for u in v] + [heat * mine[2:3]]
    flux_rows = block_transpose(fields[1:], lane)
    viscous_rows = block_transpose(viscous, lane)
    flux_high, flux_low = split(
        jnp.concatenate(
            [
                jnp.concatenate(flux_rows, axis=0),
                jnp.concatenate(
                    [fields[0]]
                    + [pltpu.roll(fields[0], 128 - 32 * g, 1) for g in range(1, 4)],
                    axis=0,
                ),
            ],
            axis=1,
        )
    )
    visc_high, visc_low = split(jnp.concatenate(viscous_rows, axis=0))

    def product(rows, columns, x_high, x_low):
        def dot(a, b):
            return jnp.dot(a[rows, columns], b, preferred_element_type=F32)

        return dot(high, x_high) + (dot(high, x_low) + dot(low, x_high))

    turned = []
    edge = []
    for g in range(4):
        rows = slice(128 * g, 128 * g + 128)
        wide = product(rows, slice(0, 512), flux_high, flux_low)
        thin = product(rows, slice(512, 1024), visc_high, visc_low)
        turned.append(wide[:, :128] + thin)
        edge.append(wide[:, 128:])
    plain = edge[0]
    for g in range(1, 4):
        plain = jnp.where(lane // 32 == g, pltpu.roll(edge[g], 32 * g, 1), plain)
    for c, value in enumerate((plain,) + tuple(block_transpose(turned, lane))):
        send[:, c] = value.reshape(NSEC, 8, 128)

    ring_near.wait_recv()

    @pl.when(jnp.logical_not(last))
    def _():
        ring_far.wait_recv()

    @pl.when(last)
    def _():
        pairs[2] = pairs[0]

    totals[sec] = pairs[1] + pairs[2]
    second = []
    for d, peer in enumerate(peers):
        second.append(
            remote(send.at[peer], back.at[sec], b_send.at[d], b_recv.at[d], ax, peer)
        )
        second.append(
            remote(
                totals.at[sec], totals.at[sec], t_send.at[d], t_recv.at[d], ax, peer
            )
        )
    for copy in second:
        copy.start()
    back[sec] = send[sec]

    for copy in halos:
        copy.wait_recv()
    planes_flux, planes_visc = [], []
    for block in (halo.at[0], q_ref, halo.at[1]):
        cells = [block[c].reshape(128, 128) for c in range(5)]
        v, pressure, heat = physical(cells)
        fields = [f.reshape(4, 32, 128) for f in flux(cells, v, pressure, 0)]
        others = [f.reshape(4, 32, 128) for f in v + [heat]]
        for plane in range(4):
            planes_flux.append([f[plane] for f in fields])
            planes_visc.append([f[plane] for f in others])
    for plane in range(4):
        at = plane + 4
        for c in range(5):
            value = out_ref[c, plane]
            for k in range(1, 5):
                weight = -TIME_STEP * FIRST_COEFFS[k - 1] / AXIAL_STEP
                value = value + weight * (
                    planes_flux[at + k][c] - planes_flux[at - k][c]
                )
            if c:
                factor = (CONDUCTION if c == 4 else VISCOSITY) * TIME_STEP
                factor = factor / (AXIAL_STEP * AXIAL_STEP)
                value = value + factor * SECOND_CENTER * planes_visc[at][c - 1]
                for k in range(1, 5):
                    value = value + factor * SECOND_COEFFS[k - 1] * (
                        planes_visc[at + k][c - 1] + planes_visc[at - k][c - 1]
                    )
            out_ref[c, plane] = value

    for copy in second:
        copy.wait_recv()
    total = totals[0]
    for s in range(1, NSEC):
        total = total + totals[s]
    bulk = jnp.sum(total, axis=1, keepdims=True) * scale
    forcing = (TIME_STEP * FORCE_RATE) * (TARGET_BULK - bulk)
    ret = [
        jnp.stack([back[4 * p + quarter] for p in range(4)]).reshape(160, 128)
        for quarter in range(4)
    ]
    for g, value in enumerate(block_transpose(ret, lane)):
        value = value.reshape(4, 5, 8, 128)
        rows = slice(8 * g, 8 * g + 8)
        for c in range(5):
            more = value[:, c]
            if c == 1:
                more = more + forcing.reshape(1, 1, 1)
            if c == 4:
                more = more + forcing.reshape(1, 1, 1) * (
                    q_ref[1, :, rows, :] / q_ref[0, :, rows, :]
                )
            out_ref[c, :, rows, :] = out_ref[c, :, rows, :] + more

    for copy in first + second + halos + [ring_near]:
        copy.wait_send()

    @pl.when(jnp.logical_not(last))
    def _():
        ring_far.wait_send()


def solution(mesh):
    high, low, radial, rows, quarter, scale = constants()

    def shards(balance_quantities, register):
        vmem = pl.BlockSpec(memory_space=pltpu.VMEM)
        hbm = pl.BlockSpec(memory_space=pl.ANY)
        dma = pltpu.SemaphoreType.DMA
        tendency = pl.pallas_call(
            functools.partial(body, scale),
            out_shape=jax.ShapeDtypeStruct((5, 4, 32, R), F32),
            in_specs=[vmem, hbm, hbm, vmem, vmem, vmem],
            out_specs=vmem,
            scratch_shapes=[
                pltpu.VMEM((NTH, 2 * NTH), BF16),
                pltpu.VMEM((NTH, 2 * NTH), BF16),
                pltpu.VMEM((NSEC, 5, 8, 128), F32),
                pltpu.VMEM((NSEC, 5, 8, 128), F32),
                pltpu.VMEM((NSEC, 5, 8, 128), F32),
                pltpu.VMEM((NSEC, 5, 8, 128), F32),
                pltpu.VMEM((2, 5, 4, 32, R), F32),
                pltpu.VMEM((NSEC, 1, 128), F32),
                pltpu.VMEM((3, 1, 128), F32),
                pltpu.VMEM((NSEC, 1, 128), F32),
                dma((2,)),
                dma((15,)),
                dma((15,)),
                dma((15,)),
                dma((15,)),
                dma((2,)),
                dma((2,)),
                dma((15,)),
                dma((15,)),
                dma((15,)),
                dma((15,)),
                dma((2,)),
                dma((2,)),
            ],
            compiler_params=pltpu.CompilerParams(
                collective_id=0,
                has_side_effects=True,
                vmem_limit_bytes=40 * 1024 * 1024,
            ),
        )(balance_quantities, high, low, radial, rows, quarter)
        register_new = SECTION_DECAY * register + tendency
        conserved_new = balance_quantities + SEGMENT_WEIGHT * register_new
        return conserved_new, register_new

    spec = P(None, "ax", "sec", None)
    return jax.shard_map(
        shards,
        mesh=mesh,
        in_specs=(spec, spec),
        out_specs=(spec, spec),
        check_vma=False,
    )
```

time: 227 us -> 51.8 us (0.23)
  the two profiles are of different devices: /device:TPU:1 before, /device:TPU:3 now
where the time goes in v1:
time: 51.8 us; the launch traced here: 51.5 us
  Pallas kernels  44.2 us (85%)
  local copies, waits for them, and re-layouts  5.75 us (11%)
  other arithmetic  0.93 us (2%)
  between operations  0.66 us (1%)
    pallas_call x1, Pallas kernels, shards(): pl.pallas_call(functools.partial(body, scale), out_shape=jax.ShapeDtypeSt...  44.2 us
    unnamed x14, local copies, waits for them, and re-layouts  5.75 us

profile of v1, /device:TPU:3, one launch (start us, length us, event | category | flops | bytes accessed | tf_op | source)
XLA Modules:
  0.0 51.5 jit_solution(11549982248082570812)
XLA Ops:
  0.6 0.0 copy-start.5
  0.6 0.7 %copy-done.5 = f32[8,128]{1,0:T(8,128)S(1)} copy-done((f32[8,128]{1,0:T(8,128)S(1)}, f32[8,128]{1,0:T(8,128)}, u32[]{:S(2)}) %copy-start.5) | copy-done | bytes 4120
  1.3 0.0 copy-start
  1.3 1.0 %copy-done = f32[5,4,32,128]{3,2,1,0:T(8,128)S(1)} copy-done((f32[5,4,32,128]{3,2,1,0:T(8,128)S(1)}, f32[5,4,32,128]{3,2,1,0:T(8,128)}, u32[]{:S(2)}) %copy-start) | copy-done | bytes 327704
  2.3 0.0 copy-start.1
  2.3 1.2 %copy-done.1 = bf16[512,1024]{1,0:T(8,128)(2,1)S(1)} copy-done((bf16[512,1024]{1,0:T(8,128)(2,1)S(1)}, bf16[512,1024]{1,0:T(8,128)(2,1)}, u32[]{:S(2)}) %copy-start.1) | copy-done | bytes 1048600
  3.5 0.0 copy-start.2
  3.5 1.2 %copy-done.2 = bf16[512,1024]{1,0:T(8,128)(2,1)S(1)} copy-done((bf16[512,1024]{1,0:T(8,128)(2,1)S(1)}, bf16[512,1024]{1,0:T(8,128)(2,1)}, u32[]{:S(2)}) %copy-start.2) | copy-done | bytes 1048600
  4.7 0.0 copy-start.3
  4.7 0.9 %copy-done.3 = f32[3,128,128]{2,1,0:T(8,128)S(1)} copy-done((f32[3,128,128]{2,1,0:T(8,128)S(1)}, f32[3,128,128]{2,1,0:T(8,128)}, u32[]{:S(2)}) %copy-start.3) | copy-done | bytes 196632
  5.7 0.0 copy-start.4
  5.7 0.7 %copy-done.4 = f32[4,8,128]{2,1,0:T(8,128)S(1)} copy-done((f32[4,8,128]{2,1,0:T(8,128)S(1)}, f32[4,8,128]{2,1,0:T(8,128)}, u32[]{:S(2)}) %copy-start.4) | copy-done | bytes 16408
  6.4 0.0 copy-start.6
  6.4 44.2 %shard_map.86 = f32[5,4,32,128]{3,2,1,0:T(8,128)S(1)} custom-call(f32[5,4,32,128]{3,2,1,0:T(8,128)S(1)} %copy-done, bf16[512,1024]{1,0:T(8,128)(2,1)S(1)} %copy-done.2, bf16[512,1024]{1,0:T(8,128)(2,1)S(1)} %copy-done.1, f32[3,128,128]{2,1,0:T(8,128)S(1)} %copy-done.3, f32[8,128]{1,0:T(8,128)S(1)} %copy-done.5, f32[4,8,128]{2,1,0:T(8,128)S(1)} %copy-done.4), custom_call_target="tpu_custom_call" | custom-call | tf_op jit(solution)/shard_map/pallas_call | solution.py:423
  50.6 0.0 copy-done.6
  50.6 0.9 %multiply_add_fusion = (f32[5,4,32,128]{3,2,1,0:T(8,128)}, f32[5,4,32,128]{3,2,1,0:T(8,128)}) fusion(f32[5,4,32,128]{3,2,1,0:T(8,128)S(1)} %copy-done, f32[5,4,32,128]{3,2,1,0:T(8,128)S(1)} %shard_map.86, f32[5,4,32,128]{3,2,1,0:T(8,128)S(1)} %copy-done.6), kind=kLoop, calls=%fused_computation | loop fusion | flops 327680 | bytes 1638400 | tf_op jit(solution)/shard_map/add | solution.py:460
Async XLA Ops:
  0.6 0.7 %copy-start.5 = (f32[8,128]{1,0:T(8,128)S(1)}, f32[8,128]{1,0:T(8,128)}, u32[]{:S(2)}) copy-start(f32[8,128]{1,0:T(8,128)} %constant.17.clone.rows_ref) | copy-start | bytes 12292
  1.3 1.0 %copy-start = (f32[5,4,32,128]{3,2,1,0:T(8,128)S(1)}, f32[5,4,32,128]{3,2,1,0:T(8,128)}, u32[]{:S(2)}) copy-start(f32[5,4,32,128]{3,2,1,0:T(8,128)} %q_ref.1) | copy-start | bytes 983044
  2.3 1.2 %copy-start.1 = (bf16[512,1024]{1,0:T(8,128)(2,1)S(1)}, bf16[512,1024]{1,0:T(8,128)(2,1)}, u32[]{:S(2)}) copy-start(bf16[512,1024]{1,0:T(8,128)(2,1)} %constant.15.clone.low_hbm) | copy-start | bytes 3145732
  3.5 1.2 %copy-start.2 = (bf16[512,1024]{1,0:T(8,128)(2,1)S(1)}, bf16[512,1024]{1,0:T(8,128)(2,1)}, u32[]{:S(2)}) copy-start(bf16[512,1024]{1,0:T(8,128)(2,1)} %constant.14.clone.high_hbm) | copy-start | bytes 3145732
  4.7 0.9 %copy-start.3 = (f32[3,128,128]{2,1,0:T(8,128)S(1)}, f32[3,128,128]{2,1,0:T(8,128)}, u32[]{:S(2)}) copy-start(f32[3,128,128]{2,1,0:T(8,128)} %constant.16.clone.radial_ref) | copy-start | bytes 589828
  5.7 0.7 %copy-start.4 = (f32[4,8,128]{2,1,0:T(8,128)S(1)}, f32[4,8,128]{2,1,0:T(8,128)}, u32[]{:S(2)}) copy-start(f32[4,8,128]{2,1,0:T(8,128)} %constant.18.clone.quarter_ref) | copy-start | bytes 49156
  6.4 44.2 %copy-start.6 = (f32[5,4,32,128]{3,2,1,0:T(8,128)S(1)}, f32[5,4,32,128]{3,2,1,0:T(8,128)}, u32[]{:S(2)}) copy-start(f32[5,4,32,128]{3,2,1,0:T(8,128)} %param.8) | copy-start | bytes 983044

commit v2 on v1

--- a/solution.py
+++ b/solution.py
@@ -55,12 +55,9 @@
         -np.pi * np.pi / (3.0 * step * step) - 1.0 / 6.0,
         -0.5 * sign / np.sin(safe * step / 2) ** 2,
     )
-    order = (
-        np.arange(NTH).reshape(NSEC, 4, 8).transpose(1, 0, 2).reshape(NTH)
-    )
-    both = np.concatenate(
-        [azim_first[order][:, order], azim_second[order][:, order]], axis=1
-    )
+    order = np.arange(NTH).reshape(4, 2, 2, 4, 8).transpose(1, 3, 0, 2, 4).reshape(NTH)
+    both = np.stack([azim_first[order][:, order], azim_second[order][:, order]])
+    both = both.reshape(2, 2, 256, 2, 256).transpose(1, 3, 0, 2, 4)
     both = both.astype(np.float32)
     high = both.astype(ml_dtypes.bfloat16)
     low = (both - high.astype(np.float32)).astype(ml_dtypes.bfloat16)
@@ -123,15 +120,19 @@
 
 def body(
     scale,
-    q_ref,
+    q_hbm,
     high_hbm,
     low_hbm,
+    radial_hbm,
+    rows_hbm,
+    quarter_hbm,
+    out_ref,
+    q_ref,
+    high,
+    low,
     radial_ref,
     rows_ref,
     quarter_ref,
-    out_ref,
-    high,
-    low,
     pack,
     recv,
     send,
@@ -153,15 +154,13 @@
     t_recv,
     h_send,
     h_recv,
+    halo_ready,
+    ring_ready,
 ):
     ax = lax.axis_index("ax")
     sec = lax.axis_index("sec")
-    loads = [
-        pltpu.make_async_copy(high_hbm, high, load_sem.at[0]),
-        pltpu.make_async_copy(low_hbm, low, load_sem.at[1]),
-    ]
-    for copy in loads:
-        copy.start()
+    x, half, core = sec // 4, lax.rem(sec // 2, 2), lax.rem(sec, 2)
+    me = 8 * half + 2 * x + core
 
     def remote(src, dst, send_sem, recv_sem, to_ax, to_sec):
         return pltpu.make_async_remote_copy(
@@ -173,28 +172,91 @@
             device_id_type=MESH,
         )
 
+    def at_sector(to_x, to_half, to_core):
+        return 4 * to_x + 2 * to_half + to_core, 8 * to_half + 2 * to_x + to_core
+
+    def shifted(dx):
+        return lax.rem(x + dx, 4)
+
+    far_peers = [
+        at_sector(shifted(dx), 1 - half, c) for c in range(2) for dx in (2, 1, 3, 0)
+    ]
+    near_peers = [
+        at_sector(shifted(dx), half, c) for c in range(2) for dx in (2, 1, 3)
+    ] + [at_sector(x, half, 1 - core)]
+    ordered = far_peers[:4] + near_peers[:3] + far_peers[4:] + near_peers[3:]
+
+    plane_at = lax.rem(ax, 8)
     right = lax.rem(ax + 1, NAX)
     left = lax.rem(ax + NAX - 1, NAX)
-    near, far = 2 * sec + 1, 2 * sec + 2
-    last = sec == NSEC - 1
+
+    def rank(at):
+        return 4 * lax.rem(at, 8) + at // 8
+
+    mine_rank = rank(ax)
+    offsets = [2 * sec + 1, 2 * sec + 2]
+    valid = [sec >= 0, sec < NSEC - 1]
+    targets = [lax.rem(ax + 2 * NAX - o, NAX) for o in offsets]
+    sources = [lax.rem(ax + o, NAX) for o in offsets]
+    target_lower = [rank(t) < mine_rank for t in targets]
+    source_lower = [rank(t) < mine_rank for t in sources]
+
+    def both(a, b):
+        return jnp.logical_and(a, b)
+
+    def signal(sem, to_ax, to_sec):
+        pl.semaphore_signal(
+            sem, inc=1, device_id=(to_ax, to_sec), device_id_type=MESH
+        )
 
     barrier = pltpu.get_barrier_semaphore()
-
-    def greet(to_ax, to_sec):
-        pl.semaphore_signal(
-            barrier, inc=1, device_id=(to_ax, to_sec), device_id_type=MESH
-        )
-
-    peers = [lax.rem(sec + d, NSEC) for d in range(1, NSEC)]
-    for peer in peers:
-        greet(ax, peer)
-    greet(left, sec)
-    greet(right, sec)
-    greet(lax.rem(ax + near, NAX), sec)
-
-    @pl.when(jnp.logical_not(last))
-    def _():
-        greet(lax.rem(ax + far, NAX), sec)
+    loads = [
+        pltpu.make_async_copy(src, dst, load_sem.at[i])
+        for i, (src, dst) in enumerate(
+            (
+                (q_hbm, q_ref),
+                (rows_hbm, rows_ref),
+                (quarter_hbm, quarter_ref),
+                (radial_hbm, radial_ref),
+                (high_hbm, high),
+                (low_hbm, low),
+            )
+        )
+    ]
+    loads[0].start()
+    loads[1].start()
+    for peer, _ in ordered:
+        signal(barrier, ax, peer)
+
+    @pl.when(plane_at != 7)
+    def _():
+        signal(barrier, right, sec)
+
+    @pl.when(plane_at == 0)
+    def _():
+        signal(barrier, left, sec)
+
+    count = 15 + jnp.where(plane_at != 0, 1, 0) + jnp.where(plane_at == 7, 1, 0)
+    for k in range(2):
+
+        @pl.when(both(valid[k], jnp.logical_not(target_lower[k])))
+        def _():
+            signal(barrier, targets[k], sec)
+
+        @pl.when(both(valid[k], jnp.logical_not(source_lower[k])))
+        def _():
+            signal(barrier, sources[k], sec)
+
+        count = count + jnp.where(both(valid[k], target_lower[k]), 1, 0)
+        count = count + jnp.where(both(valid[k], source_lower[k]), 1, 0)
+    for copy in loads[2:]:
+        copy.start()
+
+    loads[0].wait()
+    loads[1].wait()
+    radius = rows_ref[0:1, :]
+    flow = jnp.sum(q_ref[1].reshape(128, 128) * radius, axis=0, keepdims=True)
+    sums[me] = flow
 
     lane = lax.broadcasted_iota(jnp.int32, (1, 128), 1)
     groups = [
@@ -205,30 +267,65 @@
         for plane in range(4):
             pack[4 * plane + quarter] = packed[:, plane]
 
-    radius = rows_ref[0:1, :]
-    flow = jnp.sum(q_ref[1].reshape(128, 128) * radius, axis=0, keepdims=True)
-    sums[sec] = flow
-
-    pl.semaphore_wait(barrier, jnp.where(last, 18, 19))
-
-    first = []
-    for d, peer in enumerate(peers):
-        first.append(
-            remote(sums.at[sec], sums.at[sec], s_send.at[d], s_recv.at[d], ax, peer)
-        )
-        first.append(
-            remote(pack.at[peer], recv.at[sec], a_send.at[d], a_recv.at[d], ax, peer)
-        )
-    for copy in first:
-        copy.start()
-    recv[sec] = pack[sec]
-    halos = [
-        remote(q_ref, halo.at[0], h_send.at[0], h_recv.at[0], right, sec),
-        remote(q_ref, halo.at[1], h_send.at[1], h_recv.at[1], left, sec),
-    ]
-    for copy in halos:
-        copy.start()
-
+    pl.semaphore_wait(barrier, count)
+
+    def sums_copy(peer, at):
+        return remote(sums.at[me], sums.at[me], s_send.at[at], s_recv.at[me], ax, peer)
+
+    def sums_from(at):
+        return remote(sums.at[at], sums.at[at], s_send.at[at], s_recv.at[at], ax, sec)
+
+    def pack_copy(peer, at):
+        return remote(pack.at[at], recv.at[me], a_send.at[at], a_recv.at[me], ax, peer)
+
+    def pack_from(at):
+        return remote(pack.at[at], recv.at[at], a_send.at[at], a_recv.at[at], ax, sec)
+
+    def back_copy(peer, at):
+        return remote(send.at[at], back.at[me], b_send.at[at], b_recv.at[me], ax, peer)
+
+    def back_from(at):
+        return remote(send.at[at], back.at[at], b_send.at[at], b_recv.at[at], ax, sec)
+
+    def total_copy(peer, at):
+        return remote(
+            totals.at[me], totals.at[me], t_send.at[at], t_recv.at[me], ax, peer
+        )
+
+    def total_from(at):
+        return remote(
+            totals.at[at], totals.at[at], t_send.at[at], t_recv.at[at], ax, sec
+        )
+
+    for peer, at in ordered:
+        sums_copy(peer, at).start()
+    for peer, at in ordered:
+        pack_copy(peer, at).start()
+
+    @pl.when(plane_at != 0)
+    def _():
+        signal(halo_ready.at[0], left, sec)
+
+    @pl.when(plane_at == 7)
+    def _():
+        signal(halo_ready.at[1], right, sec)
+
+    for k in range(2):
+
+        @pl.when(both(valid[k], source_lower[k]))
+        def _():
+            signal(ring_ready.at[k], sources[k], sec)
+
+    to_right = remote(q_ref, halo.at[0], h_send.at[0], h_recv.at[0], right, sec)
+    to_left = remote(q_ref, halo.at[1], h_send.at[1], h_recv.at[1], left, sec)
+
+    @pl.when(plane_at != 0)
+    def _():
+        to_left.start()
+
+    recv[me] = pack[me]
+
+    loads[3].wait()
     whole = [q_ref[c].reshape(128, 128) for c in range(5)]
     v, pressure, heat = physical(whole)
     inverse_radius = rows_ref[1:2, :]
@@ -252,107 +349,131 @@
     for c in range(5):
         out_ref[c] = tend[c].reshape(4, 32, 128)
 
-    for copy in first[0::2]:
-        copy.wait_recv()
+    @pl.when(plane_at != 7)
+    def _():
+        pl.semaphore_wait(halo_ready.at[0], 1)
+
+    to_right.start()
+
+    for _, at in ordered:
+        sums_from(at).wait_recv()
     slab = sums[0]
     for s in range(1, NSEC):
         slab = slab + sums[s]
     pairs[0] = slab
-    ring_near = remote(
-        pairs.at[0],
-        pairs.at[1],
-        p_send.at[0],
-        p_recv.at[0],
-        lax.rem(ax + NAX - near, NAX),
-        sec,
-    )
-    ring_far = remote(
-        pairs.at[0],
-        pairs.at[2],
-        p_send.at[1],
-        p_recv.at[1],
-        lax.rem(ax + 2 * NAX - far, NAX),
-        sec,
-    )
-    ring_near.start()
-
-    @pl.when(jnp.logical_not(last))
-    def _():
-        ring_far.start()
-
-    for copy in loads:
-        copy.wait()
-    for copy in first[1::2]:
-        copy.wait_recv()
-    lines = [recv[:, c].reshape(128, 128) for c in range(5)]
-    v, pressure, heat = physical(lines)
-    mine = quarter_ref[lax.rem(sec, 4)]
-    fields = [f * mine[0:1] for f in flux(lines, v, pressure, 1)]
-    viscous = [u * mine[1:2] for u in v] + [heat * mine[2:3]]
-    flux_rows = block_transpose(fields[1:], lane)
-    viscous_rows = block_transpose(viscous, lane)
-    flux_high, flux_low = split(
-        jnp.concatenate(
+    ring = [
+        remote(
+            pairs.at[0],
+            pairs.at[1 + k],
+            p_send.at[k],
+            p_recv.at[k],
+            targets[k],
+            sec,
+        )
+        for k in range(2)
+    ]
+    for k in range(2):
+
+        @pl.when(both(valid[k], target_lower[k]))
+        def _():
+            ring[k].start()
+
+    loads[2].wait()
+    loads[4].wait()
+    loads[5].wait()
+    mine = quarter_ref[lax.rem(me, 4)]
+
+    def columns(which):
+        lines = recv[pl.ds(8 * which, 8)]
+        lines = [lines[:, c].reshape(64, 128) for c in range(5)]
+        v, pressure, heat = physical(lines)
+        fields = [f * mine[0:1] for f in flux(lines, v, pressure, 1)]
+        viscous = [u * mine[1:2] for u in v] + [heat * mine[2:3]]
+        shifts = [fields[0]] + [
+            pltpu.roll(fields[0], 128 - 32 * g, 1) for g in range(1, 4)
+        ]
+        wide = jnp.concatenate(
             [
-                jnp.concatenate(flux_rows, axis=0),
-                jnp.concatenate(
-                    [fields[0]]
-                    + [pltpu.roll(fields[0], 128 - 32 * g, 1) for g in range(1, 4)],
-                    axis=0,
-                ),
+                jnp.concatenate(block_transpose(fields[1:], lane), axis=0),
+                jnp.concatenate(shifts, axis=0),
             ],
             axis=1,
         )
-    )
-    visc_high, visc_low = split(jnp.concatenate(viscous_rows, axis=0))
-
-    def product(rows, columns, x_high, x_low):
-        def dot(a, b):
-            return jnp.dot(a[rows, columns], b, preferred_element_type=F32)
-
-        return dot(high, x_high) + (dot(high, x_low) + dot(low, x_high))
-
-    turned = []
-    edge = []
-    for g in range(4):
-        rows = slice(128 * g, 128 * g + 128)
-        wide = product(rows, slice(0, 512), flux_high, flux_low)
-        thin = product(rows, slice(512, 1024), visc_high, visc_low)
-        turned.append(wide[:, :128] + thin)
-        edge.append(wide[:, 128:])
-    plain = edge[0]
-    for g in range(1, 4):
-        plain = jnp.where(lane // 32 == g, pltpu.roll(edge[g], 32 * g, 1), plain)
-    for c, value in enumerate((plain,) + tuple(block_transpose(turned, lane))):
-        send[:, c] = value.reshape(NSEC, 8, 128)
-
-    ring_near.wait_recv()
-
-    @pl.when(jnp.logical_not(last))
-    def _():
-        ring_far.wait_recv()
-
-    @pl.when(last)
+        thin = jnp.concatenate(block_transpose(viscous, lane), axis=0)
+        return split(wide), split(thin)
+
+    def product(rows, which, inputs):
+        parts = []
+        for order, (x_high, x_low) in enumerate(inputs):
+            a_high = high[rows, which, order]
+            a_low = low[rows, which, order]
+
+            def dot(a, b):
+                return jnp.dot(a, b, preferred_element_type=F32)
+
+            parts.append(
+                dot(a_high, x_high) + (dot(a_high, x_low) + dot(a_low, x_high))
+            )
+        wide, thin = parts
+        return wide[:, :128] + thin, wide[:, 128:]
+
+    def deliver(rows, main, edge):
+        main = [main[64 * g : 64 * g + 64] for g in range(4)]
+        edge = [edge[64 * g : 64 * g + 64] for g in range(4)]
+        plain = edge[0]
+        for g in range(1, 4):
+            plain = jnp.where(
+                lane // 32 == g, pltpu.roll(edge[g], 32 * g, 1), plain
+            )
+        for c, value in enumerate((plain,) + tuple(block_transpose(main, lane))):
+            send[pl.ds(8 * rows, 8), c] = value.reshape(8, 8, 128)
+
+    for _, at in near_peers:
+        pack_from(at).wait_recv()
+    inputs = columns(half)
+    far_main, far_edge = product(1 - half, half, inputs)
+    near_main, near_edge = product(half, half, inputs)
+    for _, at in far_peers:
+        pack_from(at).wait_recv()
+    inputs = columns(1 - half)
+    main, edge = product(1 - half, 1 - half, inputs)
+    deliver(1 - half, far_main + main, far_edge + edge)
+    for peer, at in far_peers:
+        back_copy(peer, at).start()
+    main, edge = product(half, 1 - half, inputs)
+    deliver(half, near_main + main, near_edge + edge)
+    for peer, at in near_peers:
+        back_copy(peer, at).start()
+    back[me] = send[me]
+
+    for k in range(2):
+
+        @pl.when(both(valid[k], jnp.logical_not(target_lower[k])))
+        def _():
+            pl.semaphore_wait(ring_ready.at[k], 1)
+            ring[k].start()
+
+    @pl.when(plane_at == 0)
+    def _():
+        pl.semaphore_wait(halo_ready.at[1], 1)
+        to_left.start()
+
+    ring[0].wait_recv()
+
+    @pl.when(valid[1])
+    def _():
+        ring[1].wait_recv()
+
+    @pl.when(jnp.logical_not(valid[1]))
     def _():
         pairs[2] = pairs[0]
 
-    totals[sec] = pairs[1] + pairs[2]
-    second = []
-    for d, peer in enumerate(peers):
-        second.append(
-            remote(send.at[peer], back.at[sec], b_send.at[d], b_recv.at[d], ax, peer)
-        )
-        second.append(
-            remote(
-                totals.at[sec], totals.at[sec], t_send.at[d], t_recv.at[d], ax, peer
-            )
-        )
-    for copy in second:
-        copy.start()
-    back[sec] = send[sec]
-
-    for copy in halos:
-        copy.wait_recv()
+    totals[me] = pairs[1] + pairs[2]
+    for peer, at in ordered:
+        total_copy(peer, at).start()
+
+    to_right.wait_recv()
+    to_left.wait_recv()
     planes_flux, planes_visc = [], []
     for block in (halo.at[0], q_ref, halo.at[1]):
         cells = [block[c].reshape(128, 128) for c in range(5)]
@@ -381,8 +502,10 @@
                     )
             out_ref[c, plane] = value
 
-    for copy in second:
-        copy.wait_recv()
+    for _, at in near_peers + far_peers:
+        back_from(at).wait_recv()
+    for _, at in ordered:
+        total_from(at).wait_recv()
     total = totals[0]
     for s in range(1, NSEC):
         total = total + totals[s]
@@ -405,12 +528,18 @@
                 )
             out_ref[c, :, rows, :] = out_ref[c, :, rows, :] + more
 
-    for copy in first + second + halos + [ring_near]:
-        copy.wait_send()
-
-    @pl.when(jnp.logical_not(last))
-    def _():
-        ring_far.wait_send()
+    for peer, at in ordered:
+        sums_copy(peer, at).wait_send()
+        pack_copy(peer, at).wait_send()
+        back_copy(peer, at).wait_send()
+        total_copy(peer, at).wait_send()
+    to_right.wait_send()
+    to_left.wait_send()
+    ring[0].wait_send()
+
+    @pl.when(valid[1])
+    def _():
+        ring[1].wait_send()
 
 
 def solution(mesh):
@@ -418,44 +547,46 @@
 
     def shards(balance_quantities, register):
         vmem = pl.BlockSpec(memory_space=pltpu.VMEM)
-        hbm = pl.BlockSpec(memory_space=pl.ANY)
+        hbm = pl.BlockSpec(memory_space=pltpu.HBM)
         dma = pltpu.SemaphoreType.DMA
+        chunk = pltpu.VMEM((NSEC, 5, 8, 128), F32)
+        line = pltpu.VMEM((NSEC, 1, 128), F32)
+        each = dma((NSEC,))
+        operands = (balance_quantities, high, low, radial, rows, quarter)
         tendency = pl.pallas_call(
             functools.partial(body, scale),
             out_shape=jax.ShapeDtypeStruct((5, 4, 32, R), F32),
-            in_specs=[vmem, hbm, hbm, vmem, vmem, vmem],
+            in_specs=[hbm] * 6,
             out_specs=vmem,
-            scratch_shapes=[
-                pltpu.VMEM((NTH, 2 * NTH), BF16),
-                pltpu.VMEM((NTH, 2 * NTH), BF16),
-                pltpu.VMEM((NSEC, 5, 8, 128), F32),
-                pltpu.VMEM((NSEC, 5, 8, 128), F32),
-                pltpu.VMEM((NSEC, 5, 8, 128), F32),
-                pltpu.VMEM((NSEC, 5, 8, 128), F32),
+            scratch_shapes=[pltpu.VMEM(o.shape, o.dtype) for o in operands]
+            + [chunk] * 4
+            + [
                 pltpu.VMEM((2, 5, 4, 32, R), F32),
-                pltpu.VMEM((NSEC, 1, 128), F32),
+                line,
                 pltpu.VMEM((3, 1, 128), F32),
-                pltpu.VMEM((NSEC, 1, 128), F32),
-                dma((2,)),
-                dma((15,)),
-                dma((15,)),
-                dma((15,)),
-                dma((15,)),
+                line,
+                dma((6,)),
+                each,
+                each,
+                each,
+                each,
                 dma((2,)),
                 dma((2,)),
-                dma((15,)),
-                dma((15,)),
-                dma((15,)),
-                dma((15,)),
+                each,
+                each,
+                each,
+                each,
                 dma((2,)),
                 dma((2,)),
+                pltpu.SemaphoreType.REGULAR((2,)),
+                pltpu.SemaphoreType.REGULAR((2,)),
             ],
             compiler_params=pltpu.CompilerParams(
                 collective_id=0,
                 has_side_effects=True,
-                vmem_limit_bytes=40 * 1024 * 1024,
+                vmem_limit_bytes=60 * 1024 * 1024,
             ),
-        )(balance_quantities, high, low, radial, rows, quarter)
+        )(*operands)
         register_new = SECTION_DECAY * register + tendency
         conserved_new = balance_quantities + SEGMENT_WEIGHT * register_new
         return conserved_new, register_new

time: 51.8 us -> 43.8 us (0.85)
  the two profiles are of different devices: /device:TPU:3 before, /device:TPU:1 now
where the time goes in v2:
time: 43.8 us; the launch traced here: 43.7 us
  Pallas kernels  41.1 us (94%)
  other arithmetic  1.9 us (4%)
  between operations  0.67 us (2%)
    pallas_call x1, Pallas kernels, shards(): pl.pallas_call(functools.partial(body, scale), out_shape=jax.ShapeDtypeSt...  41.1 us
    add x1, other arithmetic, shards(): conserved_new = balance_quantities + SEGMENT_WEIGHT * register_new  1.9 us

profile of v2, /device:TPU:1, one launch (start us, length us, event | category | flops | bytes accessed | tf_op | source)
XLA Modules:
  0.0 43.7 jit_solution(2446389536182775600)
XLA Ops:
  0.6 0.0 copy-start
  0.6 0.0 copy-start.1
  0.6 41.1 %shard_map.86 = f32[5,4,32,128]{3,2,1,0:T(8,128)} custom-call(f32[5,4,32,128]{3,2,1,0:T(8,128)} %q_hbm.1, bf16[2,2,2,256,256]{4,3,2,1,0:T(8,128)(2,1)} %constant.14.clone.high_hbm, bf16[2,2,2,256,256]{4,3,2,1,0:T(8,128)(2,1)} %constant.15.clone.low_hbm, f32[3,128,128]{2,1,0:T(8,128)} %constant.16.clone.radial_hbm, f32[8,128]{1,0:T(8,128)} %constant.17.clone.rows_hbm, ...), custom_call_target="tpu_custom_call" | custom-call | tf_op jit(solution)/shard_map/pallas_call | solution.py:556
  41.8 0.0 copy-done
  41.8 0.0 copy-done.1
  41.8 1.9 %multiply_add_fusion = (f32[5,4,32,128]{3,2,1,0:T(8,128)}, f32[5,4,32,128]{3,2,1,0:T(8,128)}) fusion(f32[5,4,32,128]{3,2,1,0:T(8,128)S(1)} %copy-done, f32[5,4,32,128]{3,2,1,0:T(8,128)} %shard_map.86, f32[5,4,32,128]{3,2,1,0:T(8,128)S(1)} %copy-done.1), kind=kLoop, calls=%fused_computation | loop fusion | flops 327680 | bytes 1638400 | tf_op jit(solution)/shard_map/add | solution.py:591
Async XLA Ops:
  0.6 41.1 %copy-start = (f32[5,4,32,128]{3,2,1,0:T(8,128)S(1)}, f32[5,4,32,128]{3,2,1,0:T(8,128)}, u32[]{:S(2)}) copy-start(f32[5,4,32,128]{3,2,1,0:T(8,128)} %q_hbm.1) | copy-start | bytes 983044
  0.6 41.1 %copy-start.1 = (f32[5,4,32,128]{3,2,1,0:T(8,128)S(1)}, f32[5,4,32,128]{3,2,1,0:T(8,128)}, u32[]{:S(2)}) copy-start(f32[5,4,32,128]{3,2,1,0:T(8,128)} %param.8) | copy-start | bytes 983044

commit v3 on v2

--- a/solution.py
+++ b/solution.py
@@ -139,15 +139,12 @@
     back,
     halo,
     sums,
-    pairs,
-    totals,
+    slabs,
     load_sem,
     a_send,
     a_recv,
     s_send,
     s_recv,
-    p_send,
-    p_recv,
     b_send,
     b_recv,
     t_send,
@@ -155,7 +152,7 @@
     h_send,
     h_recv,
     halo_ready,
-    ring_ready,
+    slab_ready,
 ):
     ax = lax.axis_index("ax")
     sec = lax.axis_index("sec")
@@ -193,16 +190,13 @@
     def rank(at):
         return 4 * lax.rem(at, 8) + at // 8
 
+    def ranked(at):
+        return 8 * lax.rem(at, 4) + at // 4
+
     mine_rank = rank(ax)
-    offsets = [2 * sec + 1, 2 * sec + 2]
-    valid = [sec >= 0, sec < NSEC - 1]
-    targets = [lax.rem(ax + 2 * NAX - o, NAX) for o in offsets]
-    sources = [lax.rem(ax + o, NAX) for o in offsets]
-    target_lower = [rank(t) < mine_rank for t in targets]
-    source_lower = [rank(t) < mine_rank for t in sources]
-
-    def both(a, b):
-        return jnp.logical_and(a, b)
+
+    def each_rank(low, high, action):
+        lax.fori_loop(low, high, lambda r, _: (action(ranked(r)), 0)[1], 0)
 
     def signal(sem, to_ax, to_sec):
         pl.semaphore_signal(
@@ -228,27 +222,7 @@
     for peer, _ in ordered:
         signal(barrier, ax, peer)
 
-    @pl.when(plane_at != 7)
-    def _():
-        signal(barrier, right, sec)
-
-    @pl.when(plane_at == 0)
-    def _():
-        signal(barrier, left, sec)
-
-    count = 15 + jnp.where(plane_at != 0, 1, 0) + jnp.where(plane_at == 7, 1, 0)
-    for k in range(2):
-
-        @pl.when(both(valid[k], jnp.logical_not(target_lower[k])))
-        def _():
-            signal(barrier, targets[k], sec)
-
-        @pl.when(both(valid[k], jnp.logical_not(source_lower[k])))
-        def _():
-            signal(barrier, sources[k], sec)
-
-        count = count + jnp.where(both(valid[k], target_lower[k]), 1, 0)
-        count = count + jnp.where(both(valid[k], source_lower[k]), 1, 0)
+    each_rank(mine_rank + 1, NAX, lambda to: signal(barrier, to, sec))
     for copy in loads[2:]:
         copy.start()
 
@@ -256,7 +230,7 @@
     loads[1].wait()
     radius = rows_ref[0:1, :]
     flow = jnp.sum(q_ref[1].reshape(128, 128) * radius, axis=0, keepdims=True)
-    sums[me] = flow
+    slabs[ax] = flow
 
     lane = lax.broadcasted_iota(jnp.int32, (1, 128), 1)
     groups = [
@@ -267,7 +241,7 @@
         for plane in range(4):
             pack[4 * plane + quarter] = packed[:, plane]
 
-    pl.semaphore_wait(barrier, count)
+    pl.semaphore_wait(barrier, 15 + mine_rank)
 
     def sums_copy(peer, at):
         return remote(sums.at[me], sums.at[me], s_send.at[at], s_recv.at[me], ax, peer)
@@ -287,18 +261,16 @@
     def back_from(at):
         return remote(send.at[at], back.at[at], b_send.at[at], b_recv.at[at], ax, sec)
 
-    def total_copy(peer, at):
-        return remote(
-            totals.at[me], totals.at[me], t_send.at[at], t_recv.at[me], ax, peer
-        )
-
-    def total_from(at):
-        return remote(
-            totals.at[at], totals.at[at], t_send.at[at], t_recv.at[at], ax, sec
-        )
-
-    for peer, at in ordered:
-        sums_copy(peer, at).start()
+    def slab_copy(to):
+        return remote(slabs.at[ax], slabs.at[ax], t_send.at[to], t_recv.at[ax], to, sec)
+
+    def slab_from(to):
+        return remote(slabs.at[to], slabs.at[to], t_send.at[to], t_recv.at[to], to, sec)
+
+    to_right = remote(q_ref, halo.at[0], h_send.at[0], h_recv.at[0], right, sec)
+    to_left = remote(q_ref, halo.at[1], h_send.at[1], h_recv.at[1], left, sec)
+    each_rank(0, mine_rank, lambda to: slab_copy(to).start())
+
     for peer, at in ordered:
         pack_copy(peer, at).start()
 
@@ -310,19 +282,11 @@
     def _():
         signal(halo_ready.at[1], right, sec)
 
-    for k in range(2):
-
-        @pl.when(both(valid[k], source_lower[k]))
-        def _():
-            signal(ring_ready.at[k], sources[k], sec)
-
-    to_right = remote(q_ref, halo.at[0], h_send.at[0], h_recv.at[0], right, sec)
-    to_left = remote(q_ref, halo.at[1], h_send.at[1], h_recv.at[1], left, sec)
-
     @pl.when(plane_at != 0)
     def _():
         to_left.start()
 
+    each_rank(0, mine_rank, lambda to: signal(slab_ready, to, sec))
     recv[me] = pack[me]
 
     loads[3].wait()
@@ -352,31 +316,7 @@
     @pl.when(plane_at != 7)
     def _():
         pl.semaphore_wait(halo_ready.at[0], 1)
-
-    to_right.start()
-
-    for _, at in ordered:
-        sums_from(at).wait_recv()
-    slab = sums[0]
-    for s in range(1, NSEC):
-        slab = slab + sums[s]
-    pairs[0] = slab
-    ring = [
-        remote(
-            pairs.at[0],
-            pairs.at[1 + k],
-            p_send.at[k],
-            p_recv.at[k],
-            targets[k],
-            sec,
-        )
-        for k in range(2)
-    ]
-    for k in range(2):
-
-        @pl.when(both(valid[k], target_lower[k]))
-        def _():
-            ring[k].start()
+        to_right.start()
 
     loads[2].wait()
     loads[4].wait()
@@ -433,11 +373,29 @@
     inputs = columns(half)
     far_main, far_edge = product(1 - half, half, inputs)
     near_main, near_edge = product(half, half, inputs)
+
+    @pl.when(mine_rank < NAX - 1)
+    def _():
+        pl.semaphore_wait(slab_ready, NAX - 1 - mine_rank)
+
+    each_rank(mine_rank + 1, NAX, lambda to: slab_copy(to).start())
+    for peer, at in ordered:
+        pack_copy(peer, at).wait_send()
+
+    @pl.when(plane_at == 7)
+    def _():
+        to_right.start()
+
     for _, at in far_peers:
         pack_from(at).wait_recv()
     inputs = columns(1 - half)
     main, edge = product(1 - half, 1 - half, inputs)
     deliver(1 - half, far_main + main, far_edge + edge)
+
+    @pl.when(plane_at == 7)
+    def _():
+        to_right.wait_send()
+
     for peer, at in far_peers:
         back_copy(peer, at).start()
     main, edge = product(half, 1 - half, inputs)
@@ -446,31 +404,21 @@
         back_copy(peer, at).start()
     back[me] = send[me]
 
-    for k in range(2):
-
-        @pl.when(both(valid[k], jnp.logical_not(target_lower[k])))
-        def _():
-            pl.semaphore_wait(ring_ready.at[k], 1)
-            ring[k].start()
+    each_rank(0, mine_rank, lambda to: slab_from(to).wait_recv())
+    each_rank(mine_rank + 1, NAX, lambda to: slab_from(to).wait_recv())
+    total = slabs[0]
+    for s in range(1, NAX):
+        total = total + slabs[s]
+    sums[me] = total
+    for peer, at in ordered:
+        sums_copy(peer, at).start()
+    for peer, at in ordered:
+        back_copy(peer, at).wait_send()
 
     @pl.when(plane_at == 0)
     def _():
         pl.semaphore_wait(halo_ready.at[1], 1)
         to_left.start()
-
-    ring[0].wait_recv()
-
-    @pl.when(valid[1])
-    def _():
-        ring[1].wait_recv()
-
-    @pl.when(jnp.logical_not(valid[1]))
-    def _():
-        pairs[2] = pairs[0]
-
-    totals[me] = pairs[1] + pairs[2]
-    for peer, at in ordered:
-        total_copy(peer, at).start()
 
     to_right.wait_recv()
     to_left.wait_recv()
@@ -505,10 +453,10 @@
     for _, at in near_peers + far_peers:
         back_from(at).wait_recv()
     for _, at in ordered:
-        total_from(at).wait_recv()
-    total = totals[0]
+        sums_from(at).wait_recv()
+    total = sums[0]
     for s in range(1, NSEC):
-        total = total + totals[s]
+        total = total + sums[s]
     bulk = jnp.sum(total, axis=1, keepdims=True) * scale
     forcing = (TIME_STEP * FORCE_RATE) * (TARGET_BULK - bulk)
     ret = [
@@ -530,16 +478,14 @@
 
     for peer, at in ordered:
         sums_copy(peer, at).wait_send()
-        pack_copy(peer, at).wait_send()
-        back_copy(peer, at).wait_send()
-        total_copy(peer, at).wait_send()
-    to_right.wait_send()
+
+    @pl.when(plane_at != 7)
+    def _():
+        to_right.wait_send()
+
     to_left.wait_send()
-    ring[0].wait_send()
-
-    @pl.when(valid[1])
-    def _():
-        ring[1].wait_send()
+    each_rank(0, mine_rank, lambda to: slab_copy(to).wait_send())
+    each_rank(mine_rank + 1, NAX, lambda to: slab_copy(to).wait_send())
 
 
 def solution(mesh):
@@ -550,7 +496,6 @@
         hbm = pl.BlockSpec(memory_space=pltpu.HBM)
         dma = pltpu.SemaphoreType.DMA
         chunk = pltpu.VMEM((NSEC, 5, 8, 128), F32)
-        line = pltpu.VMEM((NSEC, 1, 128), F32)
         each = dma((NSEC,))
         operands = (balance_quantities, high, low, radial, rows, quarter)
         tendency = pl.pallas_call(
@@ -562,24 +507,21 @@
             + [chunk] * 4
             + [
                 pltpu.VMEM((2, 5, 4, 32, R), F32),
-                line,
-                pltpu.VMEM((3, 1, 128), F32),
-                line,
+                pltpu.VMEM((NSEC, 1, 128), F32),
+                pltpu.VMEM((NAX, 1, 128), F32),
                 dma((6,)),
                 each,
                 each,
                 each,
                 each,
-                dma((2,)),
-                dma((2,)),
                 each,
                 each,
-                each,
-                each,
+                dma((NAX,)),
+                dma((NAX,)),
                 dma((2,)),
                 dma((2,)),
                 pltpu.SemaphoreType.REGULAR((2,)),
-                pltpu.SemaphoreType.REGULAR((2,)),
+                pltpu.SemaphoreType.REGULAR,
             ],
             compiler_params=pltpu.CompilerParams(
                 collective_id=0,

time: 43.8 us -> 42.3 us (0.966)
  the two profiles are of different devices: /device:TPU:1 before, /device:TPU:48 now
where the time goes in v3:
time: 42.3 us; the launch traced here: 42.1 us
  Pallas kernels  39.5 us (93%)
  other arithmetic  1.9 us (4%)
  between operations  0.67 us (2%)
    pallas_call x1, Pallas kernels, shards(): pl.pallas_call(functools.partial(body, scale), out_shape=jax.ShapeDtypeSt...  39.5 us
    add x1, other arithmetic, shards(): conserved_new = balance_quantities + SEGMENT_WEIGHT * register_new  1.9 us

profile of v3, /device:TPU:48, one launch (start us, length us, event | category | flops | bytes accessed | tf_op | source)
XLA Modules:
  0.0 42.1 jit_solution(5956231577290702190)
XLA Ops:
  0.6 0.0 copy-start
  0.6 0.0 copy-start.1
  0.6 39.5 %shard_map.86 = f32[5,4,32,128]{3,2,1,0:T(8,128)} custom-call(f32[5,4,32,128]{3,2,1,0:T(8,128)} %q_hbm.1, bf16[2,2,2,256,256]{4,3,2,1,0:T(8,128)(2,1)} %constant.14.clone.high_hbm, bf16[2,2,2,256,256]{4,3,2,1,0:T(8,128)(2,1)} %constant.15.clone.low_hbm, f32[3,128,128]{2,1,0:T(8,128)} %constant.16.clone.radial_hbm, f32[8,128]{1,0:T(8,128)} %constant.17.clone.rows_hbm, ...), custom_call_target="tpu_custom_call" | custom-call | tf_op jit(solution)/shard_map/pallas_call | solution.py:501
  40.2 0.0 copy-done
  40.2 0.0 copy-done.1
  40.2 1.9 %multiply_add_fusion = (f32[5,4,32,128]{3,2,1,0:T(8,128)}, f32[5,4,32,128]{3,2,1,0:T(8,128)}) fusion(f32[5,4,32,128]{3,2,1,0:T(8,128)S(1)} %copy-done, f32[5,4,32,128]{3,2,1,0:T(8,128)} %shard_map.86, f32[5,4,32,128]{3,2,1,0:T(8,128)S(1)} %copy-done.1), kind=kLoop, calls=%fused_computation | loop fusion | flops 327680 | bytes 1638400 | tf_op jit(solution)/shard_map/add | solution.py:533
Async XLA Ops:
  0.6 39.6 %copy-start = (f32[5,4,32,128]{3,2,1,0:T(8,128)S(1)}, f32[5,4,32,128]{3,2,1,0:T(8,128)}, u32[]{:S(2)}) copy-start(f32[5,4,32,128]{3,2,1,0:T(8,128)} %q_hbm.1) | copy-start | bytes 983044
  0.6 39.6 %copy-start.1 = (f32[5,4,32,128]{3,2,1,0:T(8,128)S(1)}, f32[5,4,32,128]{3,2,1,0:T(8,128)}, u32[]{:S(2)}) copy-start(f32[5,4,32,128]{3,2,1,0:T(8,128)} %param.8) | copy-start | bytes 983044

commit v4 on v3

--- a/solution.py
+++ b/solution.py
@@ -138,6 +138,7 @@
     send,
     back,
     halo,
+    relay,
     sums,
     slabs,
     load_sem,
@@ -149,8 +150,12 @@
     b_recv,
     t_send,
     t_recv,
+    p_send,
     h_send,
     h_recv,
+    r_send,
+    r_recv,
+    f_send,
     halo_ready,
     slab_ready,
 ):
@@ -242,6 +247,11 @@
             pack[4 * plane + quarter] = packed[:, plane]
 
     pl.semaphore_wait(barrier, 15 + mine_rank)
+    each_rank(0, mine_rank, lambda to: signal(slab_ready, to, sec))
+
+    @pl.when(plane_at == 7)
+    def _():
+        signal(halo_ready.at[1], right, sec)
 
     def sums_copy(peer, at):
         return remote(sums.at[me], sums.at[me], s_send.at[at], s_recv.at[me], ax, peer)
@@ -264,29 +274,46 @@
     def slab_copy(to):
         return remote(slabs.at[ax], slabs.at[ax], t_send.at[to], t_recv.at[ax], to, sec)
 
+    def proxy_copy(to):
+        return remote(
+            slabs.at[left], slabs.at[left], p_send.at[to], t_recv.at[left], to, sec
+        )
+
     def slab_from(to):
         return remote(slabs.at[to], slabs.at[to], t_send.at[to], t_recv.at[to], to, sec)
 
     to_right = remote(q_ref, halo.at[0], h_send.at[0], h_recv.at[0], right, sec)
     to_left = remote(q_ref, halo.at[1], h_send.at[1], h_recv.at[1], left, sec)
+    second_core = core == 1
+    pass_on = remote(q_ref, relay, r_send, r_recv, right, sec)
+    carry = remote(q_ref, relay, r_send, r_recv, lax.rem(ax + NAX - 7, NAX), sec)
+    forward_right = remote(
+        relay, halo.at[0], f_send, h_recv.at[0], lax.rem(ax + 8, NAX), sec
+    )
+    forward_left = remote(
+        relay, halo.at[1], f_send, h_recv.at[1], lax.rem(ax + NAX - 2, NAX), sec
+    )
+
+    def at_plane(where, which):
+        return jnp.logical_and(plane_at == where, which)
+
     each_rank(0, mine_rank, lambda to: slab_copy(to).start())
 
     for peer, at in ordered:
         pack_copy(peer, at).start()
 
+    @pl.when(at_plane(7, second_core))
+    def _():
+        carry.start()
+
     @pl.when(plane_at != 0)
     def _():
         signal(halo_ready.at[0], left, sec)
 
-    @pl.when(plane_at == 7)
-    def _():
-        signal(halo_ready.at[1], right, sec)
-
     @pl.when(plane_at != 0)
     def _():
         to_left.start()
 
-    each_rank(0, mine_rank, lambda to: signal(slab_ready, to, sec))
     recv[me] = pack[me]
 
     loads[3].wait()
@@ -316,7 +343,18 @@
     @pl.when(plane_at != 7)
     def _():
         pl.semaphore_wait(halo_ready.at[0], 1)
+
+    @pl.when(plane_at == 0)
+    def _():
+        slab_copy(right).start()
+
+    @pl.when(plane_at != 7)
+    def _():
         to_right.start()
+
+    @pl.when(at_plane(0, second_core))
+    def _():
+        pass_on.start()
 
     loads[2].wait()
     loads[4].wait()
@@ -374,15 +412,27 @@
     far_main, far_edge = product(1 - half, half, inputs)
     near_main, near_edge = product(half, half, inputs)
 
-    @pl.when(mine_rank < NAX - 1)
-    def _():
+    def slabs_to_later():
         pl.semaphore_wait(slab_ready, NAX - 1 - mine_rank)
-
-    each_rank(mine_rank + 1, NAX, lambda to: slab_copy(to).start())
+        each_rank(mine_rank + 1, NAX, lambda to: slab_copy(to).start())
+
+    @pl.when(plane_at == 1)
+    def _():
+        slab_from(left).wait_recv()
+        each_rank(mine_rank - 3, mine_rank, lambda to: proxy_copy(to).start())
+
+    @pl.when(jnp.logical_and(plane_at != 0, mine_rank < NAX - 1))
+    def _():
+        slabs_to_later()
+
+    @pl.when(plane_at == 1)
+    def _():
+        each_rank(mine_rank + 1, NAX, lambda to: proxy_copy(to).start())
+
     for peer, at in ordered:
         pack_copy(peer, at).wait_send()
 
-    @pl.when(plane_at == 7)
+    @pl.when(at_plane(7, core == 0))
     def _():
         to_right.start()
 
@@ -392,7 +442,8 @@
     main, edge = product(1 - half, 1 - half, inputs)
     deliver(1 - half, far_main + main, far_edge + edge)
 
-    @pl.when(plane_at == 7)
+
+    @pl.when(at_plane(7, core == 0))
     def _():
         to_right.wait_send()
 
@@ -404,7 +455,13 @@
         back_copy(peer, at).start()
     back[me] = send[me]
 
-    each_rank(0, mine_rank, lambda to: slab_from(to).wait_recv())
+    gap = jnp.where(plane_at == 1, 4, 0)
+    each_rank(0, mine_rank - gap, lambda to: slab_from(to).wait_recv())
+    each_rank(
+        mine_rank + jnp.where(plane_at == 1, -3, 1),
+        mine_rank,
+        lambda to: slab_from(to).wait_recv(),
+    )
     each_rank(mine_rank + 1, NAX, lambda to: slab_from(to).wait_recv())
     total = slabs[0]
     for s in range(1, NAX):
@@ -412,13 +469,27 @@
     sums[me] = total
     for peer, at in ordered:
         sums_copy(peer, at).start()
+
+    @pl.when(at_plane(0, second_core))
+    def _():
+        carry.wait_recv()
+        forward_right.start()
+
     for peer, at in ordered:
         back_copy(peer, at).wait_send()
 
     @pl.when(plane_at == 0)
     def _():
         pl.semaphore_wait(halo_ready.at[1], 1)
+
+    @pl.when(at_plane(0, core == 0))
+    def _():
         to_left.start()
+
+    @pl.when(at_plane(1, second_core))
+    def _():
+        pass_on.wait_recv()
+        forward_left.start()
 
     to_right.wait_recv()
     to_left.wait_recv()
@@ -483,9 +554,42 @@
     def _():
         to_right.wait_send()
 
-    to_left.wait_send()
+
+    @pl.when(jnp.logical_or(plane_at != 0, core == 0))
+    def _():
+        to_left.wait_send()
+
+    @pl.when(at_plane(0, second_core))
+    def _():
+        pass_on.wait_send()
+
+    @pl.when(at_plane(7, second_core))
+    def _():
+        carry.wait_send()
+
+    @pl.when(at_plane(0, second_core))
+    def _():
+        forward_right.wait_send()
+
+    @pl.when(at_plane(1, second_core))
+    def _():
+        forward_left.wait_send()
+
     each_rank(0, mine_rank, lambda to: slab_copy(to).wait_send())
-    each_rank(mine_rank + 1, NAX, lambda to: slab_copy(to).wait_send())
+
+    @pl.when(plane_at == 0)
+    def _():
+        pl.semaphore_wait(slab_ready, NAX - 1 - mine_rank)
+        slab_copy(right).wait_send()
+
+    @pl.when(plane_at != 0)
+    def _():
+        each_rank(mine_rank + 1, NAX, lambda to: slab_copy(to).wait_send())
+
+    @pl.when(plane_at == 1)
+    def _():
+        each_rank(mine_rank - 3, mine_rank, lambda to: proxy_copy(to).wait_send())
+        each_rank(mine_rank + 1, NAX, lambda to: proxy_copy(to).wait_send())
 
 
 def solution(mesh):
@@ -507,6 +611,7 @@
             + [chunk] * 4
             + [
                 pltpu.VMEM((2, 5, 4, 32, R), F32),
+                pltpu.VMEM((5, 4, 32, R), F32),
                 pltpu.VMEM((NSEC, 1, 128), F32),
                 pltpu.VMEM((NAX, 1, 128), F32),
                 dma((6,)),
@@ -518,8 +623,12 @@
                 each,
                 dma((NAX,)),
                 dma((NAX,)),
+                dma((NAX,)),
                 dma((2,)),
                 dma((2,)),
+                dma,
+                dma,
+                dma,
                 pltpu.SemaphoreType.REGULAR((2,)),
                 pltpu.SemaphoreType.REGULAR,
             ],

time: 42.3 us -> 41.5 us (0.981)
  the two profiles are of different devices: /device:TPU:48 before, /device:TPU:1 now
where the time goes in v4:
time: 41.5 us; the launch traced here: 41 us
  Pallas kernels  38.4 us (93%)
  other arithmetic  1.9 us (5%)
  between operations  0.67 us (2%)
    pallas_call x1, Pallas kernels, shards(): pl.pallas_call(functools.partial(body, scale), out_shape=jax.ShapeDtypeSt...  38.4 us
    add x1, other arithmetic, shards(): conserved_new = balance_quantities + SEGMENT_WEIGHT * register_new  1.9 us

profile of v4, /device:TPU:1, one launch (start us, length us, event | category | flops | bytes accessed | tf_op | source)
XLA Modules:
  0.0 41.0 jit_solution(14671740654964759737)
XLA Ops:
  0.6 0.0 copy-start
  0.6 0.0 copy-start.1
  0.6 38.4 %shard_map.86 = f32[5,4,32,128]{3,2,1,0:T(8,128)} custom-call(f32[5,4,32,128]{3,2,1,0:T(8,128)} %q_hbm.1, bf16[2,2,2,256,256]{4,3,2,1,0:T(8,128)(2,1)} %constant.14.clone.high_hbm, bf16[2,2,2,256,256]{4,3,2,1,0:T(8,128)(2,1)} %constant.15.clone.low_hbm, f32[3,128,128]{2,1,0:T(8,128)} %constant.16.clone.radial_hbm, f32[8,128]{1,0:T(8,128)} %constant.17.clone.rows_hbm, ...), custom_call_target="tpu_custom_call" | custom-call | tf_op jit(solution)/shard_map/pallas_call | solution.py:605
  39.0 0.0 copy-done
  39.0 0.0 copy-done.1
  39.1 1.9 %multiply_add_fusion = (f32[5,4,32,128]{3,2,1,0:T(8,128)}, f32[5,4,32,128]{3,2,1,0:T(8,128)}) fusion(f32[5,4,32,128]{3,2,1,0:T(8,128)S(1)} %copy-done, f32[5,4,32,128]{3,2,1,0:T(8,128)} %shard_map.86, f32[5,4,32,128]{3,2,1,0:T(8,128)S(1)} %copy-done.1), kind=kLoop, calls=%fused_computation | loop fusion | flops 327680 | bytes 1638400 | tf_op jit(solution)/shard_map/add | solution.py:642
Async XLA Ops:
  0.6 38.4 %copy-start = (f32[5,4,32,128]{3,2,1,0:T(8,128)S(1)}, f32[5,4,32,128]{3,2,1,0:T(8,128)}, u32[]{:S(2)}) copy-start(f32[5,4,32,128]{3,2,1,0:T(8,128)} %q_hbm.1) | copy-start | bytes 983044
  0.6 38.4 %copy-start.1 = (f32[5,4,32,128]{3,2,1,0:T(8,128)S(1)}, f32[5,4,32,128]{3,2,1,0:T(8,128)}, u32[]{:S(2)}) copy-start(f32[5,4,32,128]{3,2,1,0:T(8,128)} %param.8) | copy-start | bytes 983044

commit v5 on v4

--- a/solution.py
+++ b/solution.py
@@ -186,7 +186,7 @@
     near_peers = [
         at_sector(shifted(dx), half, c) for c in range(2) for dx in (2, 1, 3)
     ] + [at_sector(x, half, 1 - core)]
-    ordered = far_peers[:4] + near_peers[:3] + far_peers[4:] + near_peers[3:]
+    ordered = far_peers + near_peers
 
     plane_at = lax.rem(ax, 8)
     right = lax.rem(ax + 1, NAX)
@@ -490,6 +490,18 @@
     def _():
         pass_on.wait_recv()
         forward_left.start()
+
+    for _, at in near_peers + far_peers:
+        back_from(at).wait_recv()
+    ret = [
+        jnp.stack([back[4 * p + quarter] for p in range(4)]).reshape(160, 128)
+        for quarter in range(4)
+    ]
+    for g, value in enumerate(block_transpose(ret, lane)):
+        value = value.reshape(4, 5, 8, 128)
+        rows = slice(8 * g, 8 * g + 8)
+        for c in range(5):
+            out_ref[c, :, rows, :] = out_ref[c, :, rows, :] + value[:, c]
 
     to_right.wait_recv()
     to_left.wait_recv()
@@ -521,8 +533,7 @@
                     )
             out_ref[c, plane] = value
 
-    for _, at in near_peers + far_peers:
-        back_from(at).wait_recv()
+    speed = q_ref[1] / q_ref[0]
     for _, at in ordered:
         sums_from(at).wait_recv()
     total = sums[0]
@@ -530,22 +541,9 @@
         total = total + sums[s]
     bulk = jnp.sum(total, axis=1, keepdims=True) * scale
     forcing = (TIME_STEP * FORCE_RATE) * (TARGET_BULK - bulk)
-    ret = [
-        jnp.stack([back[4 * p + quarter] for p in range(4)]).reshape(160, 128)
-        for quarter in range(4)
-    ]
-    for g, value in enumerate(block_transpose(ret, lane)):
-        value = value.reshape(4, 5, 8, 128)
-        rows = slice(8 * g, 8 * g + 8)
-        for c in range(5):
-            more = value[:, c]
-            if c == 1:
-                more = more + forcing.reshape(1, 1, 1)
-            if c == 4:
-                more = more + forcing.reshape(1, 1, 1) * (
-                    q_ref[1, :, rows, :] / q_ref[0, :, rows, :]
-                )
-            out_ref[c, :, rows, :] = out_ref[c, :, rows, :] + more
+    forcing = forcing.reshape(1, 1, 1)
+    out_ref[1] = out_ref[1] + forcing
+    out_ref[4] = out_ref[4] + forcing * speed
 
     for peer, at in ordered:
         sums_copy(peer, at).wait_send()

time: 41.5 us -> 41.3 us (level)
  no operation moved by 1% of the time
where the time goes in v5:
time: 41.3 us; the launch traced here: 40.7 us
  Pallas kernels  38.2 us (92%)
  other arithmetic  1.9 us (5%)
  between operations  0.67 us (2%)
    pallas_call x1, Pallas kernels, shards(): pl.pallas_call(functools.partial(body, scale), out_shape=jax.ShapeDtypeSt...  38.2 us
    add x1, other arithmetic, shards(): conserved_new = balance_quantities + SEGMENT_WEIGHT * register_new  1.9 us

profile of v5, /device:TPU:1, one launch (start us, length us, event | category | flops | bytes accessed | tf_op | source)
XLA Modules:
  0.0 40.7 jit_solution(1079001738964548418)
XLA Ops:
  0.6 0.0 copy-start
  0.6 0.0 copy-start.1
  0.6 38.2 %shard_map.86 = f32[5,4,32,128]{3,2,1,0:T(8,128)} custom-call(f32[5,4,32,128]{3,2,1,0:T(8,128)} %q_hbm.1, bf16[2,2,2,256,256]{4,3,2,1,0:T(8,128)(2,1)} %constant.14.clone.high_hbm, bf16[2,2,2,256,256]{4,3,2,1,0:T(8,128)(2,1)} %constant.15.clone.low_hbm, f32[3,128,128]{2,1,0:T(8,128)} %constant.16.clone.radial_hbm, f32[8,128]{1,0:T(8,128)} %constant.17.clone.rows_hbm, ...), custom_call_target="tpu_custom_call" | custom-call | tf_op jit(solution)/shard_map/pallas_call | solution.py:603
  38.8 0.0 copy-done
  38.8 0.0 copy-done.1
  38.8 1.9 %multiply_add_fusion = (f32[5,4,32,128]{3,2,1,0:T(8,128)}, f32[5,4,32,128]{3,2,1,0:T(8,128)}) fusion(f32[5,4,32,128]{3,2,1,0:T(8,128)S(1)} %copy-done, f32[5,4,32,128]{3,2,1,0:T(8,128)} %shard_map.86, f32[5,4,32,128]{3,2,1,0:T(8,128)S(1)} %copy-done.1), kind=kLoop, calls=%fused_computation | loop fusion | flops 327680 | bytes 1638400 | tf_op jit(solution)/shard_map/add | solution.py:640
Async XLA Ops:
  0.6 38.2 %copy-start = (f32[5,4,32,128]{3,2,1,0:T(8,128)S(1)}, f32[5,4,32,128]{3,2,1,0:T(8,128)}, u32[]{:S(2)}) copy-start(f32[5,4,32,128]{3,2,1,0:T(8,128)} %q_hbm.1) | copy-start | bytes 983044
  0.6 38.2 %copy-start.1 = (f32[5,4,32,128]{3,2,1,0:T(8,128)S(1)}, f32[5,4,32,128]{3,2,1,0:T(8,128)}, u32[]{:S(2)}) copy-start(f32[5,4,32,128]{3,2,1,0:T(8,128)} %param.8) | copy-start | bytes 983044

commit v6 on v5

--- a/solution.py
+++ b/solution.py
@@ -302,6 +302,10 @@
     for peer, at in ordered:
         pack_copy(peer, at).start()
 
+    @pl.when(at_plane(7, core == 0))
+    def _():
+        to_right.start()
+
     @pl.when(at_plane(7, second_core))
     def _():
         carry.start()
@@ -431,10 +435,6 @@
 
     for peer, at in ordered:
         pack_copy(peer, at).wait_send()
-
-    @pl.when(at_plane(7, core == 0))
-    def _():
-        to_right.start()
 
     for _, at in far_peers:
         pack_from(at).wait_recv()

time: 41.3 us -> 40.9 us (level)
  no operation moved by 1% of the time
where the time goes in v6:
time: 40.9 us; the launch traced here: 40.7 us
  Pallas kernels  38.2 us (93%)
  other arithmetic  1.9 us (5%)
  between operations  0.67 us (2%)
    pallas_call x1, Pallas kernels, shards(): pl.pallas_call(functools.partial(body, scale), out_shape=jax.ShapeDtypeSt...  38.2 us
    add x1, other arithmetic, shards(): conserved_new = balance_quantities + SEGMENT_WEIGHT * register_new  1.9 us

profile of v6, /device:TPU:1, one launch (start us, length us, event | category | flops | bytes accessed | tf_op | source)
XLA Modules:
  0.0 40.7 jit_solution(2026668789226339418)
XLA Ops:
  0.6 0.0 copy-start
  0.6 0.0 copy-start.1
  0.6 38.2 %shard_map.86 = f32[5,4,32,128]{3,2,1,0:T(8,128)} custom-call(f32[5,4,32,128]{3,2,1,0:T(8,128)} %q_hbm.1, bf16[2,2,2,256,256]{4,3,2,1,0:T(8,128)(2,1)} %constant.14.clone.high_hbm, bf16[2,2,2,256,256]{4,3,2,1,0:T(8,128)(2,1)} %constant.15.clone.low_hbm, f32[3,128,128]{2,1,0:T(8,128)} %constant.16.clone.radial_hbm, f32[8,128]{1,0:T(8,128)} %constant.17.clone.rows_hbm, ...), custom_call_target="tpu_custom_call" | custom-call | tf_op jit(solution)/shard_map/pallas_call | solution.py:603
  38.8 0.0 copy-done
  38.8 0.0 copy-done.1
  38.8 1.9 %multiply_add_fusion = (f32[5,4,32,128]{3,2,1,0:T(8,128)}, f32[5,4,32,128]{3,2,1,0:T(8,128)}) fusion(f32[5,4,32,128]{3,2,1,0:T(8,128)S(1)} %copy-done, f32[5,4,32,128]{3,2,1,0:T(8,128)} %shard_map.86, f32[5,4,32,128]{3,2,1,0:T(8,128)S(1)} %copy-done.1), kind=kLoop, calls=%fused_computation | loop fusion | flops 327680 | bytes 1638400 | tf_op jit(solution)/shard_map/add | solution.py:640
Async XLA Ops:
  0.6 38.2 %copy-start = (f32[5,4,32,128]{3,2,1,0:T(8,128)S(1)}, f32[5,4,32,128]{3,2,1,0:T(8,128)}, u32[]{:S(2)}) copy-start(f32[5,4,32,128]{3,2,1,0:T(8,128)} %q_hbm.1) | copy-start | bytes 983044
  0.6 38.2 %copy-start.1 = (f32[5,4,32,128]{3,2,1,0:T(8,128)S(1)}, f32[5,4,32,128]{3,2,1,0:T(8,128)}, u32[]{:S(2)}) copy-start(f32[5,4,32,128]{3,2,1,0:T(8,128)} %param.8) | copy-start | bytes 983044

commit v7 on v6

--- a/solution.py
+++ b/solution.py
@@ -475,9 +475,6 @@
         carry.wait_recv()
         forward_right.start()
 
-    for peer, at in ordered:
-        back_copy(peer, at).wait_send()
-
     @pl.when(plane_at == 0)
     def _():
         pl.semaphore_wait(halo_ready.at[1], 1)
@@ -547,6 +544,7 @@
 
     for peer, at in ordered:
         sums_copy(peer, at).wait_send()
+        back_copy(peer, at).wait_send()
 
     @pl.when(plane_at != 7)
     def _():

time: 40.9 us -> 40.9 us (level)
  no operation moved by 1% of the time
where the time goes in v7:
time: 40.9 us; the launch traced here: 40.8 us
  Pallas kernels  38.2 us (93%)
  other arithmetic  1.9 us (5%)
  between operations  0.67 us (2%)
    pallas_call x1, Pallas kernels, shards(): pl.pallas_call(functools.partial(body, scale), out_shape=jax.ShapeDtypeSt...  38.2 us
    add x1, other arithmetic, shards(): conserved_new = balance_quantities + SEGMENT_WEIGHT * register_new  1.9 us

profile of v7, /device:TPU:1, one launch (start us, length us, event | category | flops | bytes accessed | tf_op | source)
XLA Modules:
  0.0 40.8 jit_solution(3095200030709545992)
XLA Ops:
  0.6 0.0 copy-start
  0.6 0.0 copy-start.1
  0.6 38.2 %shard_map.86 = f32[5,4,32,128]{3,2,1,0:T(8,128)} custom-call(f32[5,4,32,128]{3,2,1,0:T(8,128)} %q_hbm.1, bf16[2,2,2,256,256]{4,3,2,1,0:T(8,128)(2,1)} %constant.14.clone.high_hbm, bf16[2,2,2,256,256]{4,3,2,1,0:T(8,128)(2,1)} %constant.15.clone.low_hbm, f32[3,128,128]{2,1,0:T(8,128)} %constant.16.clone.radial_hbm, f32[8,128]{1,0:T(8,128)} %constant.17.clone.rows_hbm, ...), custom_call_target="tpu_custom_call" | custom-call | tf_op jit(solution)/shard_map/pallas_call | solution.py:601
  38.9 0.0 copy-done
  38.9 0.0 copy-done.1
  38.9 1.9 %multiply_add_fusion = (f32[5,4,32,128]{3,2,1,0:T(8,128)}, f32[5,4,32,128]{3,2,1,0:T(8,128)}) fusion(f32[5,4,32,128]{3,2,1,0:T(8,128)S(1)} %copy-done, f32[5,4,32,128]{3,2,1,0:T(8,128)} %shard_map.86, f32[5,4,32,128]{3,2,1,0:T(8,128)S(1)} %copy-done.1), kind=kLoop, calls=%fused_computation | loop fusion | flops 327680 | bytes 1638400 | tf_op jit(solution)/shard_map/add | solution.py:638
Async XLA Ops:
  0.6 38.2 %copy-start = (f32[5,4,32,128]{3,2,1,0:T(8,128)S(1)}, f32[5,4,32,128]{3,2,1,0:T(8,128)}, u32[]{:S(2)}) copy-start(f32[5,4,32,128]{3,2,1,0:T(8,128)} %q_hbm.1) | copy-start | bytes 983044
  0.6 38.2 %copy-start.1 = (f32[5,4,32,128]{3,2,1,0:T(8,128)S(1)}, f32[5,4,32,128]{3,2,1,0:T(8,128)}, u32[]{:S(2)}) copy-start(f32[5,4,32,128]{3,2,1,0:T(8,128)} %param.8) | copy-start | bytes 983044
